TPU v7x, 32 devices: a whole 2x2x4 slice. The times are simulated.
32 devices in a mesh: dp: 16 (over z, y, x), mp: 2 (over core).
Axes of the slice: x: 2, y: 2, z: 4, core: 2. Of those that a mesh axis runs over, the one named last changes fastest.
Arguments:
- tokens: bfloat16 [9216, 768], P('dp'), may hold values from -6 to 6
- cotangent: bfloat16 [9216, 768], P('dp'), may hold values from -8 to 8
- task_mask: int32 [32, 16], P('dp'), may hold values 0 or 1
- group_ids: int32 [32, 288], P('dp'), may hold values from 0 to 4, as said below
- matrices: float32 [768, 9216], P('dp', 'mp'), may hold values from -3 to 3
- matrix_first: float32 [768, 9216], P('dp', 'mp'), may hold values from -9216 to 9216
- matrix_second: float32 [768, 9216], P('dp', 'mp'), may hold values from 0 to 9216
- matrix_average: float32 [768, 9216], P('dp', 'mp'), may hold values from -3 to 3
- norm_bias: float32 [6, 768], replicated, may hold values from -1 to 2
- norm_first: float32 [6, 768], replicated, may hold values from -9216 to 9216
- norm_second: float32 [6, 768], replicated, may hold values from 0 to 9216
- norm_average: float32 [6, 768], replicated, may hold values from -1 to 2
- column_bias: float32 [4608], P('mp'), may hold values from -3 to 3
- column_first: float32 [4608], P('mp'), may hold values from -9216 to 9216
- column_second: float32 [4608], P('mp'), may hold values from 0 to 9216
- column_average: float32 [4608], P('mp'), may hold values from -1 to 1
Outputs:
- output: bfloat16 [9216, 768], P('dp')
- input_grad: float32 [9216, 768], P('dp')
- matrix_grad: float32 [768, 9216], P('dp', 'mp')
- matrix_updated: float32 [768, 9216], P('dp', 'mp')
- matrix_moment: float32 [768, 9216], P('dp', 'mp')
- matrix_squares: float32 [768, 9216], P('dp', 'mp')
- matrix_smoothed: float32 [768, 9216], P('dp', 'mp')
- norm_grad: float32 [6, 768], replicated
- norm_updated: float32 [6, 768], replicated
- norm_moment: float32 [6, 768], replicated
- norm_squares: float32 [6, 768], replicated
- norm_smoothed: float32 [6, 768], replicated
- column_grad: float32 [4608], P('mp')
- column_updated: float32 [4608], P('mp')
- column_moment: float32 [4608], P('mp')
- column_squares: float32 [4608], P('mp')
- column_smoothed: float32 [4608], P('mp')
Inputs may be any that keep to these rules, and one draw needn't show every extreme that they name: `group_ids`: within each item the first 16 ids are 0 and the ids never fall; the rest are 2 t + 1 for the observations of timestep t followed by 2 t + 2 for its readouts, t from 0 to 1, every id present.
All inputs are finite; a program needn't handle non-finite values. No bound on the sum of `task_mask` on one device may be relied on, other than what follows from the above.
Results may differ from a plain program's by a relative error of at most 0.015.
Values may be sent and summed in bfloat16 or wider, within the bound.
A program may use at most 128 MiB of HBM per device.

v0:
```python
import jax
import jax.numpy as jnp
from jax import lax
from jax.sharding import PartitionSpec as P

D = 768
HEADS = 12
HD = 64
FF = 3072
STEP = 10


NORM_EPSILON = 1e-06
NEGATIVE = -1e30
GELU_SCALE = 0.7978845608028654
GELU_CUBIC = 0.044715
BETA_FIRST = 0.9
BETA_SECOND = 0.999
EPS_ADAM = 1e-08
RATE_MATRIX = 0.1
RATE_VECTOR = 0.3
DECAY_MATRIX = 0.1
AVERAGE_KEEP = 0.7


def layer_norm(values, gain_row, bias_row):
    center = values - jnp.mean(values, -1, keepdims=True)
    spread = jnp.mean(center * center, -1, keepdims=True)
    return center * lax.rsqrt(spread + NORM_EPSILON) * gain_row + bias_row


def gelu_tanh(values):
    inner_arg = GELU_SCALE * (values + GELU_CUBIC * values * values * values)
    return 0.5 * values * (1.0 + jnp.tanh(inner_arg))


def allowed_pairs(group_block, live_block):
    item_count = group_block.shape[0]
    seq_length = group_block.shape[1]
    task_slots = live_block.shape[1]
    key_live = jnp.concatenate(
        [live_block == 1, jnp.ones((item_count, seq_length - task_slots), dtype=bool)], axis=1
    )
    query_ids = group_block[:, :, None]
    key_ids = group_block[:, None, :]
    earlier = ((key_ids == 0) | (key_ids % 2 == 1)) & (key_ids <= query_ids)
    visible = (earlier | (key_ids == query_ids)) & key_live[:, None, :]
    return visible | jnp.eye(seq_length, dtype=bool)[None]


def block_scores(query_blk, key_blk, group_blk, live_blk):
    head_scale = key_blk.shape[-1] ** (-0.5)
    scores = (
        jnp.einsum("nqhe,nkhe->nhqk", query_blk, key_blk, preferred_element_type=jnp.float32)
        * head_scale
    )
    allowed = allowed_pairs(group_blk, live_blk)[:, None]
    return jnp.where(allowed, scores, NEGATIVE)


def attend_block(query_blk, key_blk, value_blk, group_blk, live_blk):
    scores = block_scores(query_blk, key_blk, group_blk, live_blk)
    row_peak = jnp.max(scores, -1, keepdims=True)
    row_total = jnp.sum(jnp.exp(scores - row_peak), -1, keepdims=True)
    log_total = row_peak + jnp.log(row_total)
    probs_low = jnp.exp(scores - log_total).astype(jnp.bfloat16)
    attended = jnp.einsum(
        "nhqk,nkhe->nqhe", probs_low, value_blk, preferred_element_type=jnp.float32
    )
    return (attended, log_total[..., 0])


def attend_back(query_blk, key_blk, value_blk, grad_blk, log_total, group_blk, live_blk):
    head_scale = key_blk.shape[-1] ** (-0.5)
    scores = block_scores(query_blk, key_blk, group_blk, live_blk)
    probs_full = jnp.exp(scores - log_total[..., None])
    probs_low = probs_full.astype(jnp.bfloat16)
    grad_value = jnp.einsum(
        "nhqk,nqhe->nkhe", probs_low, grad_blk, preferred_element_type=jnp.float32
    )
    grad_probs = jnp.einsum(
        "nqhe,nkhe->nhqk", grad_blk, value_blk, preferred_element_type=jnp.float32
    )
    grad_scores = probs_full * (grad_probs - jnp.sum(probs_full * grad_probs, -1, keepdims=True))
    scores_low = grad_scores.astype(jnp.bfloat16)
    grad_query = (
        jnp.einsum("nhqk,nkhe->nqhe", scores_low, key_blk, preferred_element_type=jnp.float32)
        * head_scale
    )
    grad_key = (
        jnp.einsum("nhqk,nqhe->nkhe", scores_low, query_blk, preferred_element_type=jnp.float32)
        * head_scale
    )
    return (
        grad_query.astype(jnp.bfloat16),
        grad_key.astype(jnp.bfloat16),
        grad_value.astype(jnp.bfloat16),
    )


def adam_update(weight_now, gradient, first_now, second_now, step_rate, weight_decay):
    first_new = BETA_FIRST * first_now + (1.0 - BETA_FIRST) * gradient
    second_new = BETA_SECOND * second_now + (1.0 - BETA_SECOND) * gradient * gradient
    first_fixed = first_new / (1.0 - BETA_FIRST**STEP)
    second_fixed = second_new / (1.0 - BETA_SECOND**STEP)
    weight_new = weight_now - step_rate * (
        first_fixed / (jnp.sqrt(second_fixed) + EPS_ADAM) + weight_decay * weight_now
    )
    return (weight_new, first_new, second_new)


def local(
    tokens,
    cotangent,
    task_mask,
    group_ids,
    matrices,
    matrix_first,
    matrix_second,
    matrix_average,
    norm_bias,
    norm_first,
    norm_second,
    norm_average,
    column_bias,
    column_first,
    column_second,
    column_average,
):
    tensor_size = lax.axis_size("mp")
    head_cols = D // tensor_size
    unit_cols = FF // tensor_size
    head_local = HEADS // tensor_size
    item_count = group_ids.shape[0]
    seq_length = group_ids.shape[1]
    block_count = item_count // 2
    weights = lax.all_gather(matrices.astype(jnp.bfloat16), "dp", axis=0, tiled=True)
    w_qkv = weights[:, : 3 * head_cols]
    w_out = weights[:, 3 * head_cols : 4 * head_cols]
    w_up = weights[:, 4 * head_cols : 4 * head_cols + unit_cols]
    w_down = weights[:, 4 * head_cols + unit_cols :]
    bias_query = column_bias[:head_cols]
    bias_value = column_bias[head_cols : 2 * head_cols]
    bias_unit = column_bias[2 * head_cols :]
    inputs = tokens.astype(jnp.float32)
    act_one = layer_norm(inputs, norm_bias[0], norm_bias[1]).astype(jnp.bfloat16)
    projected = jnp.dot(act_one, w_qkv, preferred_element_type=jnp.float32)
    query_low = (projected[:, :head_cols] + bias_query).astype(jnp.bfloat16)
    key_low = projected[:, head_cols : 2 * head_cols].astype(jnp.bfloat16)
    value_low = (projected[:, 2 * head_cols :] + bias_value).astype(jnp.bfloat16)

    def blocks(array):
        return array.reshape(block_count, 2, seq_length, head_local, HD)

    group_blocks = group_ids.reshape(block_count, 2, seq_length)
    live_blocks = task_mask.reshape(block_count, 2, task_mask.shape[1])
    attended, log_total = lax.map(
        lambda packed: attend_block(*packed),
        (blocks(query_low), blocks(key_low), blocks(value_low), group_blocks, live_blocks),
    )
    heads_out = attended.reshape(-1, head_cols).astype(jnp.bfloat16)
    head_part = jnp.einsum("rc,dc->rd", heads_out, w_out, preferred_element_type=jnp.float32)
    residual = (
        inputs + lax.psum(head_part.astype(jnp.bfloat16), "mp").astype(jnp.float32) + norm_bias[4]
    )
    act_two = layer_norm(residual, norm_bias[2], norm_bias[3]).astype(jnp.bfloat16)
    pre_unit = jnp.dot(act_two, w_up, preferred_element_type=jnp.float32) + bias_unit
    hidden = gelu_tanh(pre_unit).astype(jnp.bfloat16)
    unit_part = jnp.einsum("rf,df->rd", hidden, w_down, preferred_element_type=jnp.float32)
    final_sum = (
        residual + lax.psum(unit_part.astype(jnp.bfloat16), "mp").astype(jnp.float32) + norm_bias[5]
    )
    output = final_sum.astype(jnp.bfloat16)
    grad_final = cotangent.astype(jnp.float32)
    grad_down = jnp.einsum("rd,rf->df", cotangent, hidden, preferred_element_type=jnp.float32)
    grad_hidden = jnp.dot(cotangent, w_down, preferred_element_type=jnp.float32)
    unused_gelu, gelu_back = jax.vjp(gelu_tanh, pre_unit)
    grad_pre = gelu_back(grad_hidden)[0].astype(jnp.bfloat16)
    grad_up = jnp.einsum("rd,rf->df", act_two, grad_pre, preferred_element_type=jnp.float32)
    unit_input = lax.psum(
        jnp.einsum("rf,df->rd", grad_pre, w_up, preferred_element_type=jnp.float32).astype(
            jnp.bfloat16
        ),
        "mp",
    ).astype(jnp.float32)
    unused_two, norm_back_two = jax.vjp(layer_norm, residual, norm_bias[2], norm_bias[3])
    grad_res_norm, grad_gain_two, grad_shift_two = norm_back_two(unit_input)
    grad_residual = grad_final + grad_res_norm
    grad_res_low = grad_residual.astype(jnp.bfloat16)
    grad_out = jnp.einsum("rd,rc->dc", grad_res_low, heads_out, preferred_element_type=jnp.float32)
    grad_heads = jnp.dot(grad_res_low, w_out, preferred_element_type=jnp.float32).astype(
        jnp.bfloat16
    )
    grad_query, grad_key, grad_value = lax.map(
        lambda packed: attend_back(*packed),
        (
            blocks(query_low),
            blocks(key_low),
            blocks(value_low),
            blocks(grad_heads),
            log_total,
            group_blocks,
            live_blocks,
        ),
    )
    grad_query = grad_query.reshape(-1, head_cols)
    grad_key = grad_key.reshape(-1, head_cols)
    grad_value = grad_value.reshape(-1, head_cols)
    grad_proj = jnp.concatenate([grad_query, grad_key, grad_value], axis=1)
    grad_qkv = jnp.einsum("rd,rc->dc", act_one, grad_proj, preferred_element_type=jnp.float32)
    head_input = lax.psum(
        jnp.einsum("rc,dc->rd", grad_proj, w_qkv, preferred_element_type=jnp.float32).astype(
            jnp.bfloat16
        ),
        "mp",
    ).astype(jnp.float32)
    unused_one, norm_back_one = jax.vjp(layer_norm, inputs, norm_bias[0], norm_bias[1])
    grad_in_norm, grad_gain_one, grad_shift_one = norm_back_one(head_input)
    input_grad = grad_residual + grad_in_norm
    norm_local = jnp.stack(
        [
            grad_gain_one,
            grad_shift_one,
            grad_gain_two,
            grad_shift_two,
            jnp.sum(grad_residual, 0),
            jnp.sum(grad_final, 0),
        ]
    )
    column_local = jnp.concatenate(
        [
            jnp.sum(grad_query.astype(jnp.float32), 0),
            jnp.sum(grad_value.astype(jnp.float32), 0),
            jnp.sum(grad_pre.astype(jnp.float32), 0),
        ]
    )
    norm_grad, column_grad = lax.psum((norm_local, column_local), "dp")
    matrix_grad = lax.psum_scatter(
        jnp.concatenate([grad_qkv, grad_out, grad_up, grad_down], axis=1),
        "dp",
        scatter_dimension=0,
        tiled=True,
    )
    matrix_updated, matrix_moment, matrix_squares = adam_update(
        matrices, matrix_grad, matrix_first, matrix_second, RATE_MATRIX, DECAY_MATRIX
    )
    norm_updated, norm_moment, norm_squares = adam_update(
        norm_bias, norm_grad, norm_first, norm_second, RATE_VECTOR, 0.0
    )
    column_updated, column_moment, column_squares = adam_update(
        column_bias, column_grad, column_first, column_second, RATE_VECTOR, 0.0
    )
    matrix_smoothed = AVERAGE_KEEP * matrix_average + (1.0 - AVERAGE_KEEP) * matrix_updated
    norm_smoothed = AVERAGE_KEEP * norm_average + (1.0 - AVERAGE_KEEP) * norm_updated
    column_smoothed = AVERAGE_KEEP * column_average + (1.0 - AVERAGE_KEEP) * column_updated
    return (
        output,
        input_grad,
        matrix_grad,
        matrix_updated,
        matrix_moment,
        matrix_squares,
        matrix_smoothed,
        norm_grad,
        norm_updated,
        norm_moment,
        norm_squares,
        norm_smoothed,
        column_grad,
        column_updated,
        column_moment,
        column_squares,
        column_smoothed,
    )


def solution(mesh):
    placed = (
        P("dp", None),
        P("dp", None),
        P("dp", None),
        P("dp", None),
        P("dp", "mp"),
        P("dp", "mp"),
        P("dp", "mp"),
        P("dp", "mp"),
        P(),
        P(),
        P(),
        P(),
        P("mp"),
        P("mp"),
        P("mp"),
        P("mp"),
    )
    return jax.shard_map(
        local,
        mesh=mesh,
        in_specs=placed,
        out_specs=(
            P("dp", None),
            P("dp", None),
            P("dp", "mp"),
            P("dp", "mp"),
            P("dp", "mp"),
            P("dp", "mp"),
            P("dp", "mp"),
            P(),
            P(),
            P(),
            P(),
            P(),
            P("mp"),
            P("mp"),
            P("mp"),
            P("mp"),
            P("mp"),
        ),
        check_vma=False,
    )
```

profile of v0, /device:TPU:0, one launch (start us, length us, event | category | flops | bytes accessed | tf_op | source)
XLA Modules:
  0.0 488.3 jit_solution(11707092867687140625)
XLA Ops:
  7.3 2.0 convert_element_type.114
  9.5 0.6 slice_reduce_fusion
  10.3 0.4 fusion.30
  10.8 0.4 and_or_fusion
  11.2 104.3 %all-gather.2.cloned.1.call-done = bf16[768,4608]{1,0:T(8,128)(2,1)} async-done(((bf16[48,4608]{1,0:T(8,128)(2,1)}), bf16[768,4608]{1,0:T(8,128)(2,1)}) %all-gather.2.cloned.1.call-update) | async-done | bytes 7077904 | tf_op jit(solution)/shard_map/all_gather | solution.py:137
  115.5 2.9 fusion.37
  118.6 0.9 fusion.58
  119.5 0.6 reshape.188
  120.1 0.8 copy.52
  120.9 2.7 reshape.189
  123.6 1.8 copy.50
  125.3 1.7 reshape.190
  127.0 1.8 copy.51
  128.8 1.1 fusion.1
  130.0 1.2 exponential_reduce_fusion
  131.2 1.1 copy-done.1
  132.3 1.5 fusion.52
  133.8 0.6 copy.54
  134.4 0.4 convert_element_type.120
  134.8 2.8 convolution_convert_fusion
  137.9 17.4 %all-reduce.7.cloned.1.call-done = bf16[576,768]{1,0:T(8,128)(2,1)} async-done(((bf16[576,768]{1,0:T(8,128)(2,1)}), bf16[576,768]{1,0:T(8,128)(2,1)}) %all-reduce.7.cloned.1.call-update) | async-done | bytes 884752 | tf_op jit(solution)/shard_map/psum | solution.py:164
  155.3 1.6 fusion.49
  156.9 0.5 multiply_reduce_fusion.1
  157.5 3.6 convolution_add_fusion
  161.2 4.4 convert_reduce_fusion
  165.7 1.2 copy-done.44
  166.9 2.5 fusion.42
  169.5 6.4 %convolution_bitcast_fusion = f32[768,1536]{1,0:T(8,128)} fusion(bf16[576,768]{1,0:T(8,128)(2,1)S(1)} %copy-done.14, f32[576,1536]{1,0:T(8,128)} %copy-done.42), kind=kOutput, calls=%fused_computation.11 | convolution fusion | flops 1366917120 | bytes 9142272 | tf_op jit(solution)/shard_map/rd,rf->df/dot_general | solution.py:175
  175.9 5.0 %fusion.45 = bf16[576,768]{1,0:T(8,128)(2,1)} fusion(bf16[768,4608]{1,0:T(8,128)(2,1)} %all-gather.2.cloned.1.call-done, f32[576,1536]{1,0:T(8,128)S(1)} %copy-done.43), kind=kOutput, calls=%fused_computation.69 | convolution fusion | flops 1367359488 | bytes 6782976 | tf_op jit(solution)/shard_map/rf,df->rd/dot_general | solution.py:169
  180.9 9.2 %all-reduce.9.cloned.1.call-done = bf16[576,768]{1,0:T(8,128)(2,1)} async-done(((bf16[576,768]{1,0:T(8,128)(2,1)}), bf16[576,768]{1,0:T(8,128)(2,1)}) %all-reduce.9.cloned.1.call-update) | async-done | bytes 884752 | tf_op jit(solution)/shard_map/psum | solution.py:180
  190.1 2.0 convert_reduce_fusion.2
  192.2 1.3 fusion.33
  193.4 2.2 fusion.83
  195.6 2.2 convolution_convert_fusion.3
  197.9 1.7 reshape.191
  199.5 2.7 copy.56
  202.2 4.9 multiply_reduce_fusion
  207.2 1.7 multiply_convert_fusion
  208.9 0.7 convert_reduce_fusion.6
  209.9 1.8 fusion.54
  211.8 2.3 convert_reduce_fusion.5
  214.1 0.6 copy.60
  214.7 0.4 reshape.181
  215.1 0.8 constant_dynamic-update-slice_fusion.2
  215.9 0.6 copy.63
  216.5 0.4 reshape.182
  216.9 1.7 copy.66
  218.6 0.4 reshape.183
  219.0 0.8 constant_dynamic-update-slice_fusion.1
  219.9 0.9 constant_dynamic-update-slice_fusion
  220.7 4.3 fusion.39
  225.7 3.9 fusion.73
  229.6 2.4 fusion.62
  232.0 2.1 fusion.74
  234.2 5.5 %pad_maximum_fusion = f32[768,4608]{1,0:T(8,128)} fusion(f32[768,1536]{1,0:T(8,128)S(1)} %bitcast.39, f32[768,1536]{1,0:T(8,128)S(1)} %fusion.73, f32[768,384]{1,0:T(8,128)S(1)} %fusion.62, f32[768,1152]{1,0:T(8,128)S(1)} %fusion.74), kind=kLoop, calls=%fused_computation | loop fusion | flops 10616832 | bytes 28311552 | tf_op jit(solution)/shard_map/concatenate | solution.py:239
  239.9 7.2 %all-reduce.11.cloned.1.call-done = (bf16[576,768]{1,0:T(8,128)(2,1)}, bf16[576,768]{1,0:T(8,128)(2,1)}) async-done(((bf16[576,768]{1,0:T(8,128)(2,1)}, bf16[576,768]{1,0:T(8,128)(2,1)}), (bf16[576,768]{1,0:T(8,128)(2,1)}, bf16[576,768]{1,0:T(8,128)(2,1)})) %all-reduce.11.cloned.1.call-update) | async-done | bytes 1769488 | tf_op jit(solution)/shard_map/psum | solution.py:171
  247.2 1.9 convert_reduce_fusion.1
  249.1 1.1 fusion.34
  250.2 79.5 %all-reduce.1 = (f32[6,768]{1,0:T(8,128)S(1)}, f32[2304]{0:T(1024)S(1)}) all-reduce(f32[6,768]{1,0:T(8,128)S(1)} %stack.15, f32[2304]{0:T(1024)S(1)} %pad_maximum_fusion.1), channel_id=1, replica_groups=mesh['dp'=16,'mp'=2] {'dp'}, use_global_device_ids=true, to_apply=%region_22.23 | all-reduce | flops 6912 | bytes 55296 | tf_op jit(solution)/shard_map/psum | solution.py:237
  329.7 0.6 multiply_add_fusion.5
  330.4 0.6 multiply_add_fusion.3
  331.1 4.1 add_add_fusion.2
  335.2 141.6 %reduce-scatter.2.cloned.1.call-done = f32[48,4608]{1,0:T(8,128)} async-done(((f32[768,4608]{1,0:T(8,128)}), f32[48,4608]{1,0:T(8,128)}) %reduce-scatter.2.cloned.1.call-update) | async-done | bytes 884752 | tf_op jit(solution)/shard_map/reduce_scatter | solution.py:238
  476.8 4.5 multiply_add_fusion.1
  (140 shorter events, 2.2 us)
Async XLA Ops:
  7.2 2.2 copy-start.41
  7.2 2.3 copy-start.16
  7.2 2.9 copy-start
  7.2 3.5 copy-start.27
  7.2 3.6 copy-start.21
  7.2 108.3 %all-gather.2.cloned.1.call-start = ((), (), s32[]{:S(2)}) async-start(), calls=%async_computation.1 | async-start | bytes 7520256 | tf_op jit(solution)/shard_map/all_gather | solution.py:137
  9.4 145.9 %all-reduce.7.cloned.1.call-start = ((), (), s32[]{:S(2)}) async-start(), calls=%async_computation.2 | async-start | bytes 1769472 | tf_op jit(solution)/shard_map/psum | solution.py:164
  10.1 105.4 %copy-start.18 = (f32[768]{0:T(1024)}, f32[768]{0:T(1024)S(1)}, u32[]{:S(2)}) copy-start(f32[768]{0:T(1024)S(1)} %get-tuple-element.87) | copy-start | bytes 9220
  10.1 108.3 %copy-start.37 = (f32[768]{0:T(1024)}, f32[768]{0:T(1024)S(1)}, u32[]{:S(2)}) copy-start(f32[768]{0:T(1024)S(1)} %get-tuple-element.86) | copy-start | bytes 9220
  10.8 107.7 %copy-start.25 = (f32[576]{0:T(1024)}, f32[576]{0:T(1024)S(1)}, u32[]{:S(2)}) copy-start(f32[576]{0:T(1024)S(1)} %fusion.30) | copy-start | bytes 6916
  10.8 107.7 %copy-start.23 = (f32[576]{0:T(1024)}, f32[576]{0:T(1024)S(1)}, u32[]{:S(2)}) copy-start(f32[576]{0:T(1024)S(1)} %fusion.67) | copy-start | bytes 6916
  120.9 10.3 %copy-start.11 = (bf16[2,288,6,64]{1,3,2,0:T(8,128)(2,1)}, bf16[2,288,6,64]{1,3,2,0:T(8,128)(2,1)S(1)}, u32[]{:S(2)}) copy-start(bf16[2,288,6,64]{1,3,2,0:T(8,128)(2,1)S(1)} %copy.52) | copy-start | bytes 1327108
  125.3 4.6 copy-start.7
  128.8 1.2 copy-start.5
  129.9 2.3 copy-start.1
  134.8 22.1 %copy-start.9 = (bf16[576,384]{0,1:T(8,128)(2,1)}, bf16[576,384]{0,1:T(8,128)(2,1)S(1)}, u32[]{:S(2)}) copy-start(bf16[576,384]{0,1:T(8,128)(2,1)S(1)} %convert_element_type.120) | copy-start | bytes 1327108
  137.6 52.5 %all-reduce.9.cloned.1.call-start = ((), (), s32[]{:S(2)}) async-start(), calls=%async_computation.3 | async-start | bytes 1769472 | tf_op jit(solution)/shard_map/psum | solution.py:180
  155.3 1.6 copy-start.2
  155.3 2.2 copy-start.20
  155.3 2.2 copy-start.39
  156.9 4.2 slice-start.4
  157.5 3.7 copy-start.14
  157.5 3.7 slice-start.5
  161.2 4.5 copy-start.42
  165.7 1.2 copy-start.44
  169.4 77.7 %all-reduce.11.cloned.1.call-start = ((), (), s32[]{:S(2)}) async-start(), calls=%async_computation.5 | async-start | bytes 3538944 | tf_op jit(solution)/shard_map/psum | solution.py:171
  169.4 6.4 %copy-start.43 = (f32[576,1536]{1,0:T(8,128)S(1)}, f32[576,1536]{1,0:T(8,128)}, u32[]{:S(2)}) copy-start(f32[576,1536]{1,0:T(8,128)} %copy-done.42) | copy-start | bytes 10616836
  190.1 2.1 copy-start.4
  199.5 7.6 %slice-start = ((s8[5308416]{0:T(1024)(128)(4,1)}), s8[1114112]{0:T(1024)(128)(4,1)S(1)}, s32[]{:S(2)}) async-start(s8[5308416]{0:T(1024)(128)(4,1)} %bitcast.36), calls=%async_computation.6 | async-start | bytes 2228224
  202.2 4.9 %slice-start.1 = ((s8[5308416]{0:T(1024)(128)(4,1)}), s8[4194304]{0:T(1024)(128)(4,1)S(1)}, s32[]{:S(2)}) async-start(s8[5308416]{0:T(1024)(128)(4,1)} %bitcast.36), calls=%async_computation.7 | async-start | bytes 8388608
  207.1 1.7 copy-start.6
  208.8 1.1 copy-start.8
  209.9 1.8 copy-start.12
  214.1 1.9 copy-start.13
  225.0 0.7 copy-start.40
  225.0 4.5 copy-start.10
  225.0 251.8 %reduce-scatter.2.cloned.1.call-start = ((), (), s32[]{:S(2)}) async-start(), calls=%async_computation.4 | async-start | bytes 15040512 | tf_op jit(solution)/shard_map/reduce_scatter | solution.py:238
  225.7 6.3 %copy-start.15 = (bf16[576,1152]{0,1:T(8,128)(2,1)S(1)}, bf16[576,1152]{0,1:T(8,128)(2,1)}, u32[]{:S(2)}) copy-start(bf16[576,1152]{0,1:T(8,128)(2,1)} %constant_dynamic-update-slice_fusion) | copy-start | bytes 3981316
  225.7 6.3 %copy-start.19 = (f32[768]{0:T(1024)S(1)}, f32[768]{0:T(1024)}, u32[]{:S(2)}) copy-start(f32[768]{0:T(1024)} %copy-done.18) | copy-start | bytes 9220
  225.7 6.3 %copy-start.24 = (f32[576]{0:T(1024)S(1)}, f32[576]{0:T(1024)}, u32[]{:S(2)}) copy-start(f32[576]{0:T(1024)} %copy-done.23) | copy-start | bytes 6916
  225.7 6.3 %copy-start.38 = (f32[768]{0:T(1024)S(1)}, f32[768]{0:T(1024)}, u32[]{:S(2)}) copy-start(f32[768]{0:T(1024)} %copy-done.37) | copy-start | bytes 9220
  229.5 4.6 slice-start.2
  232.0 2.1 slice-start.3
  239.7 9.4 %copy-start.26 = (f32[576]{0:T(1024)S(1)}, f32[576]{0:T(1024)}, u32[]{:S(2)}) copy-start(f32[576]{0:T(1024)} %copy-done.25) | copy-start | bytes 6916
  247.1 2.0 copy-start.3
  247.1 82.6 %copy-start.22 = (f32[2304]{0:T(1024)S(1)}, f32[2304]{0:T(1024)}, u32[]{:S(2)}) copy-start(f32[2304]{0:T(1024)} %param.28) | copy-start | bytes 27652
  247.1 82.6 %copy-start.33 = (f32[2304]{0:T(1024)S(1)}, f32[2304]{0:T(1024)}, u32[]{:S(2)}) copy-start(f32[2304]{0:T(1024)} %param.31) | copy-start | bytes 27652
  247.1 82.6 %copy-start.34 = (f32[2304]{0:T(1024)S(1)}, f32[2304]{0:T(1024)}, u32[]{:S(2)}) copy-start(f32[2304]{0:T(1024)} %param.29) | copy-start | bytes 27652
  247.1 82.6 %copy-start.35 = (f32[2304]{0:T(1024)S(1)}, f32[2304]{0:T(1024)}, u32[]{:S(2)}) copy-start(f32[2304]{0:T(1024)} %param.30) | copy-start | bytes 27652
  247.1 83.2 %copy-start.17 = (f32[6,768]{1,0:T(8,128)S(1)}, f32[6,768]{1,0:T(8,128)}, u32[]{:S(2)}) copy-start(f32[6,768]{1,0:T(8,128)} %param.24) | copy-start | bytes 55300
  247.2 83.2 %copy-start.28 = (f32[6,768]{1,0:T(8,128)S(1)}, f32[6,768]{1,0:T(8,128)}, u32[]{:S(2)}) copy-start(f32[6,768]{1,0:T(8,128)} %param.27) | copy-start | bytes 55300
  247.2 83.2 %copy-start.29 = (f32[6,768]{1,0:T(8,128)S(1)}, f32[6,768]{1,0:T(8,128)}, u32[]{:S(2)}) copy-start(f32[6,768]{1,0:T(8,128)} %param.25) | copy-start | bytes 55300
  247.2 83.2 %copy-start.30 = (f32[6,768]{1,0:T(8,128)S(1)}, f32[6,768]{1,0:T(8,128)}, u32[]{:S(2)}) copy-start(f32[6,768]{1,0:T(8,128)} %param.26) | copy-start | bytes 55300
  247.2 83.9 %copy-start.32 = (f32[768]{0:T(1024)S(1)}, f32[768]{0:T(1024)}, u32[]{:S(2)}) copy-start(f32[768]{0:T(1024)} %get-tuple-element.82) | copy-start | bytes 9220
  329.7 5.5 %copy-start.31 = (f32[6,768]{1,0:T(8,128)}, f32[6,768]{1,0:T(8,128)S(1)}, u32[]{:S(2)}) copy-start(f32[6,768]{1,0:T(8,128)S(1)} %get-tuple-element.88) | copy-start | bytes 55300
  329.7 5.5 %copy-start.36 = (f32[2304]{0:T(1024)}, f32[2304]{0:T(1024)S(1)}, u32[]{:S(2)}) copy-start(f32[2304]{0:T(1024)S(1)} %get-tuple-element.89) | copy-start | bytes 27652
Sparse Core Ops, SparseCore 0:
  11.5 104.0 all-gather.1
  137.7 17.4 all-reduce.6
  169.5 20.5 all-reduce.8
  225.1 21.9 all-reduce.10
  254.3 222.4 reduce-scatter.1
where the time goes:
time: 497 us; the launch traced here: 488 us
  waiting for transfers between devices  280 us (56%)
  blocking collectives  79.5 us (16%)
  matrix products  54.9 us (11%)
  other arithmetic  32.9 us (7%)
  local copies, waits for them, and re-layouts  25.4 us (5%)
  between operations  15.1 us (3%)
    reduce_scatter x1, waiting for transfers between devices, local(): lax.psum_scatter(jnp.concatenate([grad_qkv, grad_out, grad_up, grad_down]...  142 us
    all_gather x1, waiting for transfers between devices, local(): lax.all_gather(matrices.astype(jnp.bfloat16), 'dp', axis=0, tiled=True)  104 us
    psum x1, blocking collectives, local(): norm_grad, column_grad = lax.psum((norm_local, column_local), 'dp')  79.5 us
    psum x1, waiting for transfers between devices, local(): lax.psum(head_part.astype(jnp.bfloat16), 'mp').astype(jnp.float32)  17.4 us
    squeeze x8, local copies, waits for them, and re-layouts, local(): lax.map(lambda packed: attend_block(*packed), (blocks(query_low), blocks(...  13.6 us
  transfers between devices with their start and end apart: 5, of which 5 were waited for; matrix products, arithmetic and copies ran while one was open for 7% of the time, Pallas kernels for 0%

commit v1 on v0

--- a/solution.py
+++ b/solution.py
@@ -1,7 +1,13 @@
+import functools
+
 import jax
 import jax.numpy as jnp
 from jax import lax
+from jax.experimental import pallas as pl
+from jax.experimental.pallas import tpu as pltpu
 from jax.sharding import PartitionSpec as P
+
+MESH = pl.DeviceIdType.MESH
 
 D = 768
 HEADS = 12
@@ -21,6 +27,260 @@
 RATE_VECTOR = 0.3
 DECAY_MATRIX = 0.1
 AVERAGE_KEEP = 0.7
+
+
+NZ, NY, NX = 4, 2, 2
+OUTER = NZ * NY * NX
+UNIT = 128
+
+
+class Place:
+    def __init__(self, inner):
+        index = lax.axis_index("dp")
+        outer = index // inner
+        self.inner = inner
+        self.rest = index % inner
+        self.core = lax.axis_index("mp")
+        self.x = outer % NX
+        self.y = (outer // NX) % NY
+        self.z = outer // (NX * NY)
+
+    def device(self, z, y, x):
+        return (((z * NY + y) * NX + x) * self.inner + self.rest, self.core)
+
+    def along_z(self, step):
+        return self.device((self.z + step) % NZ, self.y, self.x)
+
+    def across_y(self):
+        return self.device(self.z, 1 - self.y, self.x)
+
+    def across_x(self):
+        return self.device(self.z, self.y, 1 - self.x)
+
+    def sibling(self):
+        return (self.device(self.z, self.y, self.x)[0], 1 - self.core)
+
+    def greet(self, with_sibling):
+        barrier = pltpu.get_barrier_semaphore()
+        peers = [self.along_z(step) for step in range(1, NZ)] + [self.across_y(), self.across_x()]
+        if with_sibling:
+            peers.append(self.sibling())
+        for peer in peers:
+            pl.semaphore_signal(barrier, inc=1, device_id=peer, device_id_type=MESH)
+        pl.semaphore_wait(barrier, len(peers))
+
+
+def remote(src, dst, send_sem, recv_sem, peer):
+    return pltpu.make_async_remote_copy(
+        src_ref=src, dst_ref=dst, send_sem=send_sem, recv_sem=recv_sem, device_id=peer, device_id_type=MESH
+    )
+
+
+class Gather:
+    def __init__(self, place, full, z_send, z_recv, hop_send, hop_recv):
+        self.place, self.full = place, full
+        self.z_send, self.z_recv, self.hop_send, self.hop_recv = z_send, z_recv, hop_send, hop_recv
+
+    def z_copy(self, unit, step, owner_z):
+        p = self.place
+        block = self.full.at[owner_z, p.y, p.x, :, pl.ds(unit * UNIT, UNIT)]
+        return remote(block, block, self.z_send.at[unit, step - 1], self.z_recv.at[unit, step - 1], p.along_z(step))
+
+    def hop_copy(self, unit, hop, mine):
+        p = self.place
+        cols = pl.ds(unit * UNIT, UNIT)
+        x_first = unit % 2 == 0
+        over_x = x_first == (hop == 0)
+        y = p.y if (mine or over_x) else 1 - p.y
+        x = p.x if (mine or not over_x) else 1 - p.x
+        if hop == 0:
+            block = self.full.at[:, y, x, :, cols]
+        elif x_first:
+            block = self.full.at[:, y, :, :, cols]
+        else:
+            block = self.full.at[:, :, x, :, cols]
+        peer = p.across_x() if over_x else p.across_y()
+        return remote(block, block, self.hop_send.at[unit, hop], self.hop_recv.at[unit, hop], peer)
+
+    def start_z(self, unit):
+        for step in range(1, NZ):
+            self.z_copy(unit, step, self.place.z).start()
+
+    def start_hop(self, unit, hop):
+        if hop == 0:
+            for step in range(1, NZ):
+                self.z_copy(unit, step, (self.place.z - step) % NZ).wait_recv()
+        else:
+            self.hop_copy(unit, 0, False).wait_recv()
+        self.hop_copy(unit, hop, True).start()
+
+    def finish(self, unit):
+        self.hop_copy(unit, 1, False).wait_recv()
+
+    def drain(self, unit):
+        for step in range(1, NZ):
+            self.z_copy(unit, step, self.place.z).wait_send()
+        for hop in range(2):
+            self.hop_copy(unit, hop, True).wait_send()
+
+
+class Scatter:
+    def __init__(self, place, full, got_a, got_b, got_z, result, hop_send, hop_recv, z_send, z_recv):
+        self.place, self.full, self.got_a, self.got_b, self.got_z, self.result = place, full, got_a, got_b, got_z, result
+        self.hop_send, self.hop_recv, self.z_send, self.z_recv = hop_send, hop_recv, z_send, z_recv
+
+    def part(self, unit, hop, mine):
+        p = self.place
+        cols = pl.ds(unit * UNIT, UNIT)
+        y = p.y if mine else 1 - p.y
+        x = p.x if mine else 1 - p.x
+        if unit % 2 == 0:
+            return (slice(None), y, slice(None), slice(None), cols) if hop == 0 else (slice(None), p.y, x, slice(None), cols)
+        return (slice(None), slice(None), x, slice(None), cols) if hop == 0 else (slice(None), y, p.x, slice(None), cols)
+
+    def hop_copy(self, unit, hop):
+        p = self.place
+        over_y = (unit % 2 == 0) == (hop == 0)
+        got = (self.got_a if hop == 0 else self.got_b).at[unit]
+        return remote(
+            self.full.at[self.part(unit, hop, False)],
+            got,
+            self.hop_send.at[unit, hop],
+            self.hop_recv.at[unit, hop],
+            p.across_y() if over_y else p.across_x(),
+        )
+
+    def z_copy(self, unit, step):
+        p = self.place
+        block = self.full.at[(p.z + step) % NZ, p.y, p.x, :, pl.ds(unit * UNIT, UNIT)]
+        return remote(
+            block, self.got_z.at[unit, step - 1], self.z_send.at[unit, step - 1], self.z_recv.at[unit, step - 1], p.along_z(step)
+        )
+
+    def start(self, unit):
+        self.hop_copy(unit, 0).start()
+
+    def add(self, unit, hop):
+        self.hop_copy(unit, hop).wait_recv()
+        part = self.part(unit, hop, True)
+        got = (self.got_a if hop == 0 else self.got_b)[unit]
+        self.full[part] = (self.full[part].astype(jnp.float32) + got.astype(jnp.float32)).astype(jnp.bfloat16)
+
+    def middle(self, unit):
+        self.add(unit, 0)
+        self.hop_copy(unit, 1).start()
+
+    def last(self, unit):
+        self.add(unit, 1)
+        for step in range(1, NZ):
+            self.z_copy(unit, step).start()
+
+    def finish(self, unit):
+        p = self.place
+        cols = pl.ds(unit * UNIT, UNIT)
+        total = self.full[p.z, p.y, p.x, :, cols].astype(jnp.float32)
+        for step in range(1, NZ):
+            self.z_copy(unit, step).wait_recv()
+            total = total + self.got_z[unit, step - 1].astype(jnp.float32)
+        self.result[:, cols] = total
+
+    def drain(self, unit):
+        for hop in range(2):
+            self.hop_copy(unit, hop).wait_send()
+        for step in range(1, NZ):
+            self.z_copy(unit, step).wait_send()
+
+
+def gather_kernel(inner, units, mats, out, full, *sems):
+    place = Place(inner)
+    place.greet(False)
+    gather = Gather(place, full, *sems)
+    full[place.z, place.y, place.x] = mats[...].astype(jnp.bfloat16)
+    pairs = units // 2
+    for pair in range(min(3, pairs)):
+        gather.start_z(2 * pair)
+        gather.start_z(2 * pair + 1)
+    for t in range(pairs + LAG):
+        if t < pairs:
+            gather.start_hop(2 * t, 0)
+            gather.start_hop(2 * t + 1, 0)
+            if t + 3 < pairs:
+                gather.start_z(2 * t + 6)
+                gather.start_z(2 * t + 7)
+        if t >= LAG:
+            gather.start_hop(2 * (t - LAG), 1)
+            gather.start_hop(2 * (t - LAG) + 1, 1)
+    for unit in range(units):
+        gather.finish(unit)
+        gather.drain(unit)
+    out[...] = full[...].reshape(out.shape)
+
+
+def scatter_kernel(inner, units, grads, out, full, *rest):
+    place = Place(inner)
+    place.greet(False)
+    full[...] = grads[...].reshape(full.shape)
+    got_a, got_b, got_z, hop_send, hop_recv, z_send, z_recv = rest
+    scatter = Scatter(place, full, got_a, got_b, got_z, out, hop_send, hop_recv, z_send, z_recv)
+    pairs = units // 2
+    for t in range(pairs + 3 * LAG):
+        for part in range(2):
+            if t < pairs:
+                scatter.start(2 * t + part)
+            if 0 <= t - LAG < pairs:
+                scatter.middle(2 * (t - LAG) + part)
+            if 0 <= t - 2 * LAG < pairs:
+                scatter.last(2 * (t - 2 * LAG) + part)
+            if 0 <= t - 3 * LAG < pairs:
+                scatter.finish(2 * (t - 3 * LAG) + part)
+    for unit in range(units):
+        scatter.drain(unit)
+
+
+LAG = 2
+
+
+def gather_rows(mats, inner):
+    rows, cols = mats.shape
+    units = cols // UNIT
+    dma = pltpu.SemaphoreType.DMA
+    return pl.pallas_call(
+        functools.partial(gather_kernel, inner, units),
+        out_shape=jax.ShapeDtypeStruct((OUTER * rows, cols), jnp.bfloat16),
+        in_specs=[pl.BlockSpec(memory_space=pltpu.VMEM)],
+        out_specs=pl.BlockSpec(memory_space=pltpu.VMEM),
+        scratch_shapes=[
+            pltpu.VMEM((NZ, NY, NX, rows, cols), jnp.bfloat16),
+            dma((units, NZ - 1)),
+            dma((units, NZ - 1)),
+            dma((units, 2)),
+            dma((units, 2)),
+        ],
+        compiler_params=pltpu.CompilerParams(collective_id=0, has_side_effects=True, vmem_limit_bytes=56 << 20),
+    )(mats)
+
+
+def scatter_rows(grads, inner):
+    rows, cols = grads.shape[0] // OUTER, grads.shape[1]
+    units = cols // UNIT
+    dma = pltpu.SemaphoreType.DMA
+    return pl.pallas_call(
+        functools.partial(scatter_kernel, inner, units),
+        out_shape=jax.ShapeDtypeStruct((rows, cols), jnp.float32),
+        in_specs=[pl.BlockSpec(memory_space=pltpu.VMEM)],
+        out_specs=pl.BlockSpec(memory_space=pltpu.VMEM),
+        scratch_shapes=[
+            pltpu.VMEM((NZ, NY, NX, rows, cols), jnp.bfloat16),
+            pltpu.VMEM((units, NZ, 2, rows, UNIT), jnp.bfloat16),
+            pltpu.VMEM((units, NZ, rows, UNIT), jnp.bfloat16),
+            pltpu.VMEM((units, NZ - 1, rows, UNIT), jnp.bfloat16),
+            dma((units, 2)),
+            dma((units, 2)),
+            dma((units, NZ - 1)),
+            dma((units, NZ - 1)),
+        ],
+        compiler_params=pltpu.CompilerParams(collective_id=1, has_side_effects=True, vmem_limit_bytes=56 << 20),
+    )(grads)
 
 
 def layer_norm(values, gain_row, bias_row):
@@ -134,7 +394,14 @@
     item_count = group_ids.shape[0]
     seq_length = group_ids.shape[1]
     block_count = item_count // 2
-    weights = lax.all_gather(matrices.astype(jnp.bfloat16), "dp", axis=0, tiled=True)
+    dp_size = lax.axis_size("dp")
+    inner = dp_size // OUTER
+    if inner > 1:
+        groups = [[o * inner + i for i in range(inner)] for o in range(OUTER)]
+        slab = lax.all_gather(matrices.astype(jnp.bfloat16), "dp", axis=0, tiled=True, axis_index_groups=groups)
+    else:
+        slab = matrices
+    weights = gather_rows(slab, inner)
     w_qkv = weights[:, : 3 * head_cols]
     w_out = weights[:, 3 * head_cols : 4 * head_cols]
     w_up = weights[:, 4 * head_cols : 4 * head_cols + unit_cols]
@@ -235,12 +502,13 @@
         ]
     )
     norm_grad, column_grad = lax.psum((norm_local, column_local), "dp")
-    matrix_grad = lax.psum_scatter(
-        jnp.concatenate([grad_qkv, grad_out, grad_up, grad_down], axis=1),
-        "dp",
-        scatter_dimension=0,
-        tiled=True,
-    )
+    matrix_grad = scatter_rows(
+        jnp.concatenate([grad_qkv, grad_out, grad_up, grad_down], axis=1).astype(jnp.bfloat16), inner
+    )
+    if inner > 1:
+        matrix_grad = lax.psum_scatter(
+            matrix_grad, "dp", scatter_dimension=0, tiled=True, axis_index_groups=groups
+        )
     matrix_updated, matrix_moment, matrix_squares = adam_update(
         matrices, matrix_grad, matrix_first, matrix_second, RATE_MATRIX, DECAY_MATRIX
     )

time: 497 us -> 423 us (0.85)
  waiting for transfers between devices: 280 us -> 29.3 us
  Pallas kernels: 0 us -> 153 us
  local copies, waits for them, and re-layouts: 25.4 us -> 43.2 us
  matrix products: 54.9 us -> 62.2 us
  other arithmetic: 32.9 us -> 38.2 us
    pallas_call x0 -> x2, Pallas kernels: none -> 153 us  [the longest x1 77.2 us: gather_rows(): pl.pallas_call(functools.partial(gather_kernel, inner, units), out_shape=...]
    reduce_scatter x1 -> x0, waiting for transfers between devices: 142 us -> none  [local(): lax.psum_scatter(jnp.concatenate([grad_qkv, grad_out, grad_up, grad_down]...]
    all_gather x1 -> x0, waiting for transfers between devices: 104 us -> none  [local(): lax.all_gather(matrices.astype(jnp.bfloat16), 'dp', axis=0, tiled=True)]
    psum x1, waiting for transfers between devices: 7.21 us -> 0.01 us  [local(): lax.psum(unit_part.astype(jnp.bfloat16), 'mp').astype(jnp.float32)]
  transfers between devices with their start and end apart: 5 -> 3, of which waited for: 5 -> 2; matrix products, arithmetic and copies ran while one was open for 7% -> 7% of each run, Pallas kernels for 0% -> 18%
where the time goes in v1:
time: 423 us; the launch traced here: 417 us
  Pallas kernels  153 us (36%)
  blocking collectives  76.2 us (18%)
  matrix products  62.2 us (15%)
  local copies, waits for them, and re-layouts  43.2 us (10%)
  other arithmetic  38.2 us (9%)
  waiting for transfers between devices  29.3 us (7%)
  between operations  14.7 us (3%)
    pallas_call x1, Pallas kernels, gather_rows(): pl.pallas_call(functools.partial(gather_kernel, inner, units), out_shape=...  77.2 us
    psum x1, blocking collectives, local(): norm_grad, column_grad = lax.psum((norm_local, column_local), 'dp')  76.2 us
    pallas_call x1, Pallas kernels, scatter_rows(): pl.pallas_call(functools.partial(scatter_kernel, inner, units), out_shape...  76.1 us
    psum x1, waiting for transfers between devices, local(): lax.psum(head_part.astype(jnp.bfloat16), 'mp').astype(jnp.float32)  18.7 us
    psum x1, waiting for transfers between devices, local(): lax.psum(jnp.einsum('rf,df->rd', grad_pre, w_up, preferred_element_type=j...  10.5 us
    squeeze x8, local copies, waits for them, and re-layouts, local(): lax.map(lambda packed: attend_block(*packed), (blocks(query_low), blocks(...  9.97 us
  transfers between devices with their start and end apart: 3, of which 2 were waited for; matrix products, arithmetic and copies ran while one was open for 7% of the time, Pallas kernels for 18%

profile of v1, /device:TPU:0, one launch (start us, length us, event | category | flops | bytes accessed | tf_op | source)
XLA Modules:
  0.0 417.2 jit_solution(12943732159620093055)
XLA Ops:
  7.2 0.7 iota_compare_fusion
  7.9 1.6 slice_reduce_fusion
  9.5 1.4 convert_reduce_fusion.3
  10.9 1.6 fusion.31
  13.1 77.2 %shard_map.287 = bf16[768,4608]{1,0:T(8,128)(2,1)} custom-call(f32[48,4608]{1,0:T(8,128)} %mats.1), custom_call_target="tpu_custom_call" | custom-call | tf_op jit(solution)/shard_map/pallas_call | solution.py:247
  90.4 3.0 fusion.38
  93.4 0.9 fusion.59
  94.9 1.3 copy.50
  96.9 0.8 copy.51
  97.8 1.4 and_or_fusion
  99.2 1.2 fusion.1
  100.4 1.2 exponential_reduce_fusion
  101.6 1.1 copy-done.1
  103.4 0.8 copy.52
  104.2 4.2 %fusion.53 = bf16[2,288,6,64]{1,3,2,0:T(8,128)(2,1)S(1)} fusion(bf16[2,288,6,64]{1,3,2,0:T(8,128)(2,1)S(1)} %copy.52, f32[2,6,288,288]{2,3,1,0:T(8,128)} %copy-done.1, f32[2,6,288]{2,1,0:T(8,128)S(1)} %log_add_fusion, pred[2,288,288]{1,2,0:T(8,128)(4,1)S(1)} %and_or_fusion), kind=kOutput, calls=%fused_computation.85 | convolution fusion | flops 131604480 | bytes 5045760 | tf_op jit(solution)/shard_map/while/body/eval_jaxpr/nhqk,nkhe->nqhe/dot_general | solution.py:327
  109.5 2.8 convolution_convert_fusion.3
  112.4 18.7 %all-reduce.7.cloned.1.call-done = bf16[576,768]{1,0:T(8,128)(2,1)} async-done(((bf16[576,768]{1,0:T(8,128)(2,1)}), bf16[576,768]{1,0:T(8,128)(2,1)}) %all-reduce.7.cloned.1.call-update) | async-done | bytes 884752 | tf_op jit(solution)/shard_map/psum | solution.py:431
  131.1 1.6 fusion.50
  133.3 3.6 convolution_add_fusion
  137.0 5.2 %convert_reduce_fusion = (f32[1536]{0:T(1024)}, bf16[576,1536]{1,0:T(8,128)(2,1)S(1)}) fusion(f32[576,1536]{1,0:T(8,128)S(1)} %convolution_add_fusion, bf16[576,768]{1,0:T(8,128)(2,1)S(1)} %copy-done.20, bf16[768,4608]{1,0:T(8,128)(2,1)S(1)} %bitcast.39), kind=kOutput, calls=%fused_computation.17 | convolution fusion | flops 1381956096 | bytes 8558592 | tf_op jit(solution)/shard_map/dot_general | solution.py:443
  142.2 3.6 fusion.9
  145.9 2.5 fusion.43
  148.4 5.3 %convolution_convert_fusion.1 = bf16[768,1536]{1,0:T(8,128)(2,1)} fusion(bf16[576,1536]{1,0:T(8,128)(2,1)} %copy-done.45, f32[768]{0:T(1024)S(1)} %get-tuple-element.83, f32[768]{0:T(1024)S(1)} %get-tuple-element.84, f32[576]{0:T(1024)S(1)} %fusion.68, bf16[576,768]{1,0:T(8,128)(2,1)S(1)} %copy-done.2, bf16[576,768]{1,0:T(8,128)(2,1)S(1)} %copy-done, ...), kind=kOutput, calls=%fused_computation.21 | convolution fusion | flops 1364115456 | bytes 5912064 | tf_op jit(solution)/shard_map/rd,rf->df/dot_general | solution.py:446
  153.8 4.8 %fusion.46 = bf16[576,768]{1,0:T(8,128)(2,1)} fusion(bf16[768,4608]{1,0:T(8,128)(2,1)} %shard_map.287, f32[576,1536]{1,0:T(8,128)S(1)} %copy-done.44), kind=kOutput, calls=%fused_computation.72 | convolution fusion | flops 1367359488 | bytes 6782976 | tf_op jit(solution)/shard_map/rf,df->rd/dot_general | solution.py:436
  158.5 10.5 %all-reduce.9.cloned.1.call-done = bf16[576,768]{1,0:T(8,128)(2,1)} async-done(((bf16[576,768]{1,0:T(8,128)(2,1)}), bf16[576,768]{1,0:T(8,128)(2,1)}) %all-reduce.9.cloned.1.call-update) | async-done | bytes 884752 | tf_op jit(solution)/shard_map/psum | solution.py:447
  169.1 2.6 convert_reduce_fusion.2
  171.8 1.8 fusion.34
  173.5 2.3 fusion.81
  175.8 2.4 convolution_convert_fusion.7
  178.3 2.8 reshape.191
  181.1 2.4 copy.56
  183.5 5.0 %convert_reduce_fusion.5 = (f32[6,64]{1,0:T(8,128)}, bf16[2,288,6,64]{1,3,2,0:T(8,128)(2,1)S(1)}) fusion(bf16[2,288,6,64]{1,3,2,0:T(8,128)(2,1)} %copy.56, f32[2,6,288,288]{2,3,1,0:T(8,128)} %copy-done.1, f32[2,6,288]{2,1,0:T(8,128)} %copy-done.25, pred[2,288,288]{1,2,0:T(8,128)(4,1)} %copy-done.6), kind=kOutput, calls=%fused_computation.89 | convolution fusion | flops 132046464 | bytes 5047296 | tf_op jit(solution)/shard_map/while/body/eval_jaxpr/nhqk,nqhe->nkhe/dot_general | solution.py:338
  188.5 4.5 %multiply_reduce_fusion = (f32[2,6,288]{2,1,0:T(8,128)S(1)}, f32[2,6,288,288]{2,3,1,0:T(8,128)S(1)}) fusion(f32[2,6,288,288]{2,3,1,0:T(8,128)} %copy-done.1, f32[2,6,288]{2,1,0:T(8,128)S(1)} %copy-done.26, pred[2,288,288]{1,2,0:T(8,128)(4,1)S(1)} %copy-done.7, bf16[2,288,6,64]{1,3,2,0:T(8,128)(2,1)S(1)} %copy-done.17, bf16[2,288,6,64]{1,3,2,0:T(8,128)(2,1)S(1)} %copy-done.16), kind=kOutput, calls=%fused_computation.2 | convolution fusion | flops 132375168 | bytes 9040896 | tf_op jit(solution)/shard_map/while/body/eval_jaxpr/nqhe,nkhe->nhqk/dot_general | solution.py:341
  193.1 1.5 multiply_convert_fusion
  194.6 2.1 convert_reduce_fusion.6
  196.7 1.9 fusion.55
  198.6 1.6 convolution_convert_fusion.4
  200.2 1.4 copy.66
  201.6 2.7 reshape.183
  204.3 2.5 copy.63
  206.8 2.7 reshape.182
  209.5 2.5 copy.60
  212.0 2.9 reshape.181
  214.8 1.1 constant_dynamic-update-slice_fusion.2
  215.9 1.1 constant_dynamic-update-slice_fusion.1
  217.1 1.1 copy-done.27
  218.3 3.8 fusion.40
  222.1 4.7 %convolution_convert_fusion.2 = bf16[768,1152]{1,0:T(8,128)(2,1)} fusion(bf16[576,1152]{0,1:T(8,128)(2,1)} %copy-done.27, bf16[576,768]{1,0:T(8,128)(2,1)S(1)} %copy-done, f32[768]{0:T(1024)} %copy-done.41, f32[768]{0:T(1024)S(1)} %get-tuple-element.87, f32[576]{0:T(1024)S(1)} %copy-done.31, f32[576]{0:T(1024)S(1)} %broadcast_multiply_fusion.1), kind=kOutput, calls=%fused_computation.22 | convolution fusion | flops 1022754816 | bytes 3992064 | tf_op jit(solution)/shard_map/rd,rc->dc/dot_general | solution.py:477
  226.8 6.3 %pad_maximum_fusion.grads = bf16[768,4608]{1,0:T(8,128)(2,1)} fusion(bf16[768,1536]{1,0:T(8,128)(2,1)} %fusion.9, bf16[768,1536]{1,0:T(8,128)(2,1)} %convolution_convert_fusion.1, bf16[768,384]{1,0:T(8,128)(2,1)} %convolution_convert_fusion.4, bf16[768,1152]{1,0:T(8,128)(2,1)} %convolution_convert_fusion.2), kind=kLoop, calls=%fused_computation | loop fusion | flops 28311552 | bytes 14155776 | tf_op jit(solution)/shard_map/concatenate | solution.py:506
  233.1 1.3 reduce_sum.212
  234.4 1.3 reduce_sum.207
  235.7 1.3 stack.14
  237.0 1.3 stack.6
  238.3 1.3 reshape.186
  240.2 76.1 %shard_map.288 = f32[48,4608]{1,0:T(8,128)} custom-call(bf16[768,4608]{1,0:T(8,128)(2,1)} %pad_maximum_fusion.grads), custom_call_target="tpu_custom_call" | custom-call | tf_op jit(solution)/shard_map/pallas_call | solution.py:267
  316.9 3.5 multiply_add_fusion.1
  320.4 1.9 convert_reduce_fusion.1
  322.3 1.1 fusion.35
  325.1 1.4 stack.15
  326.5 76.2 %all-reduce.1 = (f32[6,768]{1,0:T(8,128)}, f32[2304]{0:T(1024)}) all-reduce(f32[6,768]{1,0:T(8,128)} %stack.15, f32[2304]{0:T(1024)} %pad_maximum_fusion.1), channel_id=1, replica_groups=mesh['dp'=16,'mp'=2] {'dp'}, use_global_device_ids=true, to_apply=%region_21.22 | all-reduce | flops 6912 | bytes 55296 | tf_op jit(solution)/shard_map/psum | solution.py:504
  402.7 1.5 multiply_add_fusion.3
  404.2 1.4 multiply_add_fusion.5
  405.6 4.0 add_add_fusion.2
  409.5 0.9 copy.90
  (133 shorter events, 7.6 us)
Async XLA Ops:
  7.2 123.9 %all-reduce.7.cloned.1.call-start = ((), (), s32[]{:S(2)}) async-start(), calls=%async_computation | async-start | bytes 1769472 | tf_op jit(solution)/shard_map/psum | solution.py:431
  9.5 80.8 %copy-start.41 = (f32[768]{0:T(1024)}, f32[768]{0:T(1024)S(1)}, u32[]{:S(2)}) copy-start(f32[768]{0:T(1024)S(1)} %get-tuple-element.86) | copy-start | bytes 9220
  9.5 162.2 %copy-start.28 = (f32[768]{0:T(1024)}, f32[768]{0:T(1024)S(1)}, u32[]{:S(2)}) copy-start(f32[768]{0:T(1024)S(1)} %get-tuple-element.84) | copy-start | bytes 9220
  12.5 0.6 copy-start.33
  13.1 77.3 %copy-start.30 = (f32[576]{0:T(1024)}, f32[576]{0:T(1024)S(1)}, u32[]{:S(2)}) copy-start(f32[576]{0:T(1024)S(1)} %fusion.67) | copy-start | bytes 6916
  13.1 77.2 %copy-start.29 = (f32[2304]{0:T(1024)S(1)}, f32[2304]{0:T(1024)}, u32[]{:S(2)}) copy-start(f32[2304]{0:T(1024)} %param.28) | copy-start | bytes 27652
  13.1 77.3 %copy-start = (bf16[576,768]{1,0:T(8,128)(2,1)S(1)}, bf16[576,768]{1,0:T(8,128)(2,1)}, u32[]{:S(2)}) copy-start(bf16[576,768]{1,0:T(8,128)(2,1)} %param.16) | copy-start | bytes 2654212
  96.2 3.0 copy-start.10
  96.2 1.5 copy-start.42
  96.2 1.5 copy-start.36
  97.7 2.7 copy-start.8
  99.2 5.0 %copy-start.6 = (pred[2,288,288]{1,2,0:T(8,128)(4,1)}, pred[2,288,288]{1,2,0:T(8,128)(4,1)S(1)}, u32[]{:S(2)}) copy-start(pred[2,288,288]{1,2,0:T(8,128)(4,1)S(1)} %and_or_fusion) | copy-start | bytes 497668
  100.4 2.3 copy-start.1
  100.4 2.3 copy-start.19
  102.7 5.7 %copy-start.25 = (f32[2,6,288]{2,1,0:T(8,128)}, f32[2,6,288]{2,1,0:T(8,128)S(1)}, u32[]{:S(2)}) copy-start(f32[2,6,288]{2,1,0:T(8,128)S(1)} %log_add_fusion) | copy-start | bytes 41476
  104.2 4.2 %copy-start.15 = (bf16[2,288,6,64]{1,3,2,0:T(8,128)(2,1)}, bf16[2,288,6,64]{1,3,2,0:T(8,128)(2,1)S(1)}, u32[]{:S(2)}) copy-start(bf16[2,288,6,64]{1,3,2,0:T(8,128)(2,1)S(1)} %copy.52) | copy-start | bytes 1327108
  109.5 2.9 copy-start.12
  112.3 56.8 %all-reduce.9.cloned.1.call-start = ((), (), s32[]{:S(2)}) async-start(), calls=%async_computation.1 | async-start | bytes 1769472 | tf_op jit(solution)/shard_map/psum | solution.py:447
  131.1 1.6 copy-start.2
  132.8 4.2 %slice-start.2 = ((s8[7077888]{0:T(1024)(128)(4,1)}), s8[4194304]{0:T(1024)(128)(4,1)S(1)}, s32[]{:S(2)}) async-start(s8[7077888]{0:T(1024)(128)(4,1)} %bitcast.38), calls=%async_computation.5 | async-start | bytes 8388608
  133.3 38.5 %copy-start.35 = (f32[576]{0:T(1024)}, f32[576]{0:T(1024)S(1)}, u32[]{:S(2)}) copy-start(f32[576]{0:T(1024)S(1)} %fusion.68) | copy-start | bytes 6916
  133.3 3.7 slice-start.3
  133.3 3.7 copy-start.20
  137.0 5.2 %copy-start.43 = (f32[576,1536]{1,0:T(8,128)}, f32[576,1536]{1,0:T(8,128)S(1)}, u32[]{:S(2)}) copy-start(f32[576,1536]{1,0:T(8,128)S(1)} %convolution_add_fusion) | copy-start | bytes 10616836
  142.2 3.6 copy-start.45
  148.4 172.0 %all-reduce.11.cloned.1.call-start = ((), (), s32[]{:S(2)}) async-start(), calls=%async_computation.2 | async-start | bytes 3538944 | tf_op jit(solution)/shard_map/psum | solution.py:438
  148.4 5.3 %copy-start.44 = (f32[576,1536]{1,0:T(8,128)S(1)}, f32[576,1536]{1,0:T(8,128)}, u32[]{:S(2)}) copy-start(f32[576,1536]{1,0:T(8,128)} %copy-done.43) | copy-start | bytes 10616836
  169.1 2.7 copy-start.5
  171.7 1.8 copy-start.21
  183.5 5.0 %copy-start.7 = (pred[2,288,288]{1,2,0:T(8,128)(4,1)S(1)}, pred[2,288,288]{1,2,0:T(8,128)(4,1)}, u32[]{:S(2)}) copy-start(pred[2,288,288]{1,2,0:T(8,128)(4,1)} %copy-done.6) | copy-start | bytes 497668
  183.5 5.0 %copy-start.16 = (bf16[2,288,6,64]{1,3,2,0:T(8,128)(2,1)S(1)}, bf16[2,288,6,64]{1,3,2,0:T(8,128)(2,1)}, u32[]{:S(2)}) copy-start(bf16[2,288,6,64]{1,3,2,0:T(8,128)(2,1)} %copy-done.15) | copy-start | bytes 1327108
  183.5 5.0 %copy-start.17 = (bf16[2,288,6,64]{1,3,2,0:T(8,128)(2,1)S(1)}, bf16[2,288,6,64]{1,3,2,0:T(8,128)(2,1)}, u32[]{:S(2)}) copy-start(bf16[2,288,6,64]{1,3,2,0:T(8,128)(2,1)} %copy.56) | copy-start | bytes 1327108
  183.5 5.0 %copy-start.26 = (f32[2,6,288]{2,1,0:T(8,128)S(1)}, f32[2,6,288]{2,1,0:T(8,128)}, u32[]{:S(2)}) copy-start(f32[2,6,288]{2,1,0:T(8,128)} %copy-done.25) | copy-start | bytes 41476
  183.5 9.5 %slice-start = ((s8[5308416]{0:T(1024)(128)(4,1)}), s8[4194304]{0:T(1024)(128)(4,1)S(1)}, s32[]{:S(2)}) async-start(s8[5308416]{0:T(1024)(128)(4,1)} %bitcast.36), calls=%async_computation.3 | async-start | bytes 8388608
  188.5 4.5 %slice-start.1 = ((s8[5308416]{0:T(1024)(128)(4,1)}), s8[1114112]{0:T(1024)(128)(4,1)S(1)}, s32[]{:S(2)}) async-start(s8[5308416]{0:T(1024)(128)(4,1)} %bitcast.36), calls=%async_computation.4 | async-start | bytes 2228224
  193.1 1.5 copy-start.9
  194.6 2.1 copy-start.11
  196.7 1.9 copy-start.13
  214.8 2.2 copy-start.18
  217.1 1.1 copy-start.27
  218.3 3.8 copy-start.31
  226.8 12.8 %copy-start.37 = (f32[768]{0:T(1024)S(1)}, f32[768]{0:T(1024)}, u32[]{:S(2)}) copy-start(f32[768]{0:T(1024)} %get-tuple-element.78) | copy-start | bytes 9220
  240.1 76.1 %copy-start.38 = (f32[1536]{0:T(1024)S(1)}, f32[1536]{0:T(1024)}, u32[]{:S(2)}) copy-start(f32[1536]{0:T(1024)} %get-tuple-element.117) | copy-start | bytes 18436
  240.1 76.1 %copy-start.39 = (f32[384]{0:T(512)S(1)}, f32[384]{0:T(512)}, u32[]{:S(2)}) copy-start(f32[384]{0:T(512)} %reduce_sum.212) | copy-start | bytes 4612
  240.1 76.1 %copy-start.40 = (f32[384]{0:T(512)S(1)}, f32[384]{0:T(512)}, u32[]{:S(2)}) copy-start(f32[384]{0:T(512)} %reduce_sum.207) | copy-start | bytes 4612
  240.1 76.8 %copy-start.14 = (f32[48,4608]{1,0:T(8,128)S(1)}, f32[48,4608]{1,0:T(8,128)}, u32[]{:S(2)}) copy-start(f32[48,4608]{1,0:T(8,128)} %mats.1) | copy-start | bytes 2654212
  240.1 76.8 %copy-start.22 = (f32[48,4608]{1,0:T(8,128)S(1)}, f32[48,4608]{1,0:T(8,128)}, u32[]{:S(2)}) copy-start(f32[48,4608]{1,0:T(8,128)} %param.23) | copy-start | bytes 2654212
  240.2 76.7 %copy-start.23 = (f32[48,4608]{1,0:T(8,128)S(1)}, f32[48,4608]{1,0:T(8,128)}, u32[]{:S(2)}) copy-start(f32[48,4608]{1,0:T(8,128)} %param.21) | copy-start | bytes 2654212
  240.2 76.7 %copy-start.24 = (f32[48,4608]{1,0:T(8,128)S(1)}, f32[48,4608]{1,0:T(8,128)}, u32[]{:S(2)}) copy-start(f32[48,4608]{1,0:T(8,128)} %param.22) | copy-start | bytes 2654212
  320.4 1.9 copy-start.34
  320.4 1.9 copy-start.3
  320.4 1.9 copy-start.32
  405.6 4.0 copy-start.4
Sparse Core Ops, SparseCore 0:
  112.4 18.6 all-reduce.6
  148.5 20.5 all-reduce.8
  226.9 21.9 all-reduce.10

commit v2 on v0

v2 whole, which is shorter than its diff:
```python
import functools

import jax
import jax.numpy as jnp
from jax import lax
from jax.experimental import pallas as pl
from jax.experimental.pallas import tpu as pltpu
from jax.sharding import PartitionSpec as P

MESH = pl.DeviceIdType.MESH

D = 768
HEADS = 12
HD = 64
FF = 3072
STEP = 10


NORM_EPSILON = 1e-06
NEGATIVE = -1e30
GELU_SCALE = 0.7978845608028654
GELU_CUBIC = 0.044715
BETA_FIRST = 0.9
BETA_SECOND = 0.999
EPS_ADAM = 1e-08
RATE_MATRIX = 0.1
RATE_VECTOR = 0.3
DECAY_MATRIX = 0.1
AVERAGE_KEEP = 0.7


NZ, NY, NX = 4, 2, 2
OUTER = NZ * NY * NX
ROW_TILE = 32
COL_TILE = 256
F32, BF16 = jnp.float32, jnp.bfloat16


class Place:
    def __init__(self, inner):
        index = lax.axis_index("dp")
        outer = index // inner
        self.inner = inner
        self.rest = index % inner
        self.core = lax.axis_index("mp")
        self.x = outer % NX
        self.y = (outer // NX) % NY
        self.z = outer // (NX * NY)

    def device(self, z, y, x):
        return (((z * NY + y) * NX + x) * self.inner + self.rest, self.core)

    def along_z(self, step):
        return self.device((self.z + step) % NZ, self.y, self.x)

    def across_y(self):
        return self.device(self.z, 1 - self.y, self.x)

    def across_x(self):
        return self.device(self.z, self.y, 1 - self.x)

    def sibling(self):
        return (self.device(self.z, self.y, self.x)[0], 1 - self.core)

    def greet(self):
        barrier = pltpu.get_barrier_semaphore()
        peers = [self.along_z(step) for step in range(1, NZ)]
        peers += [self.across_y(), self.across_x(), self.sibling()]
        for peer in peers:
            pl.semaphore_signal(barrier, inc=1, device_id=peer, device_id_type=MESH)
        pl.semaphore_wait(barrier, len(peers))


def remote(src, dst, send_sem, recv_sem, peer):
    return pltpu.make_async_remote_copy(
        src_ref=src,
        dst_ref=dst,
        send_sem=send_sem,
        recv_sem=recv_sem,
        device_id=peer,
        device_id_type=MESH,
    )


class Gather:
    def __init__(self, place, units, full, z_send, z_recv, hop_send, hop_recv):
        self.place, self.units, self.full = place, units, full
        self.z_send, self.z_recv, self.hop_send, self.hop_recv = z_send, z_recv, hop_send, hop_recv

    def z_copy(self, unit, step, owner_z):
        p = self.place
        block = self.full.at[owner_z, p.y, p.x, :, pl.ds(*self.units[unit])]
        return remote(
            block,
            block,
            self.z_send.at[unit, step - 1],
            self.z_recv.at[unit, step - 1],
            p.along_z(step),
        )

    def hop_copy(self, unit, hop, mine):
        p = self.place
        cols = pl.ds(*self.units[unit])
        x_first = unit % 2 == 0
        over_x = x_first == (hop == 0)
        y = p.y if (mine or over_x) else 1 - p.y
        x = p.x if (mine or not over_x) else 1 - p.x
        if hop == 0:
            block = self.full.at[:, y, x, :, cols]
        elif x_first:
            block = self.full.at[:, y, :, :, cols]
        else:
            block = self.full.at[:, :, x, :, cols]
        peer = p.across_x() if over_x else p.across_y()
        return remote(
            block, block, self.hop_send.at[unit, hop], self.hop_recv.at[unit, hop], peer
        )

    def start_z(self, unit):
        for step in range(1, NZ):
            self.z_copy(unit, step, self.place.z).start()

    def start_hop(self, unit, hop):
        if hop == 0:
            for step in range(1, NZ):
                self.z_copy(unit, step, (self.place.z - step) % NZ).wait_recv()
        else:
            self.hop_copy(unit, 0, False).wait_recv()
        self.hop_copy(unit, hop, True).start()

    def finish(self, unit):
        self.hop_copy(unit, 1, False).wait_recv()

    def drain(self, unit):
        for step in range(1, NZ):
            self.z_copy(unit, step, self.place.z).wait_send()
        for hop in range(2):
            self.hop_copy(unit, hop, True).wait_send()


class Scatter:
    def __init__(
        self, place, units, full, got_a, got_b, got_z, result, hop_send, hop_recv, z_send, z_recv
    ):
        self.place, self.units, self.full, self.result = place, units, full, result
        self.got_a, self.got_b, self.got_z = got_a, got_b, got_z
        self.hop_send, self.hop_recv, self.z_send, self.z_recv = hop_send, hop_recv, z_send, z_recv
        self.begun = 0
        self.passed = [0, 0, 0]

    def part(self, unit, hop, mine):
        p = self.place
        cols = pl.ds(*self.units[unit])
        every = slice(None)
        y = p.y if mine else 1 - p.y
        x = p.x if mine else 1 - p.x
        if unit % 2 == 0:
            return (every, y, every, every, cols) if hop == 0 else (every, p.y, x, every, cols)
        return (every, every, x, every, cols) if hop == 0 else (every, y, p.x, every, cols)

    def landing(self, unit, hop):
        cols = pl.ds(*self.units[unit])
        if hop == 0:
            return self.got_a.at[:, :, :, cols]
        return self.got_b.at[:, :, cols]

    def hop_copy(self, unit, hop):
        p = self.place
        over_y = (unit % 2 == 0) == (hop == 0)
        return remote(
            self.full.at[self.part(unit, hop, False)],
            self.landing(unit, hop),
            self.hop_send.at[unit, hop],
            self.hop_recv.at[unit, hop],
            p.across_y() if over_y else p.across_x(),
        )

    def z_copy(self, unit, step):
        p = self.place
        cols = pl.ds(*self.units[unit])
        return remote(
            self.full.at[(p.z + step) % NZ, p.y, p.x, :, cols],
            self.got_z.at[step - 1, :, cols],
            self.z_send.at[unit, step - 1],
            self.z_recv.at[unit, step - 1],
            p.along_z(step),
        )

    def add(self, unit, hop):
        self.hop_copy(unit, hop).wait_recv()
        part = self.part(unit, hop, True)
        got = self.landing(unit, hop)[...]
        self.full[part] = (self.full[part].astype(F32) + got.astype(F32)).astype(BF16)

    def start(self, unit):
        self.hop_copy(unit, 0).start()

    def middle(self, unit):
        self.add(unit, 0)
        self.hop_copy(unit, 1).start()

    def last(self, unit):
        self.add(unit, 1)
        for step in range(1, NZ):
            self.z_copy(unit, step).start()

    def finish(self, unit):
        p = self.place
        cols = pl.ds(*self.units[unit])
        total = self.full[p.z, p.y, p.x, :, cols].astype(F32)
        for step in range(1, NZ):
            self.z_copy(unit, step).wait_recv()
            total = total + self.got_z[step - 1, :, cols].astype(F32)
        self.result[:, cols] = total

    def drain(self, unit):
        for hop in range(2):
            self.hop_copy(unit, hop).wait_send()
        for step in range(1, NZ):
            self.z_copy(unit, step).wait_send()

    def begin(self, pairs):
        for pair in range(self.begun, self.begun + pairs):
            self.start(2 * pair)
            self.start(2 * pair + 1)
        self.begun += pairs

    def advance(self):
        limits = [self.begun, self.passed[0], self.passed[1]]
        for depth, stage in enumerate((self.middle, self.last, self.finish)):
            pair = self.passed[depth]
            if pair < limits[depth]:
                stage(2 * pair)
                stage(2 * pair + 1)
                self.passed[depth] += 1

    def complete(self):
        while self.passed[2] < self.begun:
            self.advance()


def rows_dot(left, right):
    return jnp.dot(left, right, preferred_element_type=F32)


def dot_rt(left, right):
    return lax.dot_general(left, right, (((1,), (1,)), ((), ())), preferred_element_type=F32)


def dot_lt(left, right):
    return lax.dot_general(left, right, (((0,), (0,)), ((), ())), preferred_element_type=F32)


def normalized(values):
    center = values - jnp.mean(values, -1, keepdims=True)
    spread = jnp.mean(center * center, -1, keepdims=True)
    scale = lax.rsqrt(spread + NORM_EPSILON)
    return center * scale, scale


def total_rows(values):
    return jnp.sum(values, 0, keepdims=True)


GATHER_UNITS = (
    [(0, 128), (128, 128), (256, 256), (512, 256), (768, 384), (1152, 384)]
    + [(1536 + 256 * i, 256) for i in range(6)]
    + [(3072 + 256 * i, 256) for i in range(6)]
)
SCATTER_UNITS = (
    [(3072 + 256 * i, 256) for i in range(6)]
    + [(1536 + 256 * i, 256) for i in range(6)]
    + [(1152, 128), (1280, 256)]
    + [(0, 256), (256, 128), (384, 256), (640, 128), (768, 128), (896, 256)]
)
HEAD_COLS, UNIT_COLS = 384, 1536
Q0, K0, V0, O0, U0, W0 = 0, 384, 768, 1152, 1536, 3072


def block_kernel(inner, items, length, tokens, cotangent, task_mask, group_ids, matrices, norm, column, *rest):
    (out, input_grad, matrix_grad, vectors) = rest[:4]
    (full, grads, got_a, got_b, got_z) = rest[4:9]
    (act_one, act_one_t, act_two, act_two_t, cot_t, proj, grad_proj, heads, grad_heads) = rest[9:18]
    (caps, probs, residual, slope, hidden, grad_pre, grad_res, grad_low, ex_send, ex_recv) = rest[18:28]
    (vec_got, vec_z) = rest[28:30]
    (gz_send, gz_recv, gh_send, gh_recv, sh_send, sh_recv, sz_send, sz_recv) = rest[30:38]
    (es, er, vs, vr) = rest[38:42]
    rows = items * length
    place = Place(inner)
    gather = Gather(place, GATHER_UNITS, full, gz_send, gz_recv, gh_send, gh_recv)
    scatter = Scatter(
        place, SCATTER_UNITS, grads, got_a, got_b, got_z, matrix_grad, sh_send, sh_recv, sz_send, sz_recv
    )
    place.greet()

    def weight(start, width):
        return full[:, :, :, :, pl.ds(start, width)].reshape(D, width)

    def put_grad(start, width, value):
        grads[:, :, :, :, pl.ds(start, width)] = value.astype(BF16).reshape(grads.shape[:4] + (width,))

    def tiles(body, carry=None):
        def step(index, value):
            return body(pl.ds(pl.multiple_of(index * ROW_TILE, ROW_TILE), ROW_TILE), value)

        return lax.fori_loop(0, rows // ROW_TILE, step, carry)

    def exchange(turn, item):
        part = pl.ds(item * length, length)
        slot = turn % 2
        return remote(
            ex_send.at[slot, part],
            ex_recv.at[slot, part],
            es.at[turn, item],
            er.at[turn, item],
            place.sibling(),
        )

    def send_part(turn, item, value):
        if turn >= 2:
            exchange(turn - 2, item).wait_send()
        ex_send[turn % 2, pl.ds(item * length, length)] = value.astype(BF16)
        exchange(turn, item).start()

    def wait_part(turn):
        for item in range(items):
            exchange(turn, item).wait_recv()

    def both(turn, tile):
        return ex_send[turn % 2, tile].astype(F32) + ex_recv[turn % 2, tile].astype(F32)

    pairs = len(GATHER_UNITS) // 2
    ahead = 2

    def cast_pair(pair):
        for unit in (2 * pair, 2 * pair + 1):
            cols = pl.ds(*GATHER_UNITS[unit])
            full[place.z, place.y, place.x, :, cols] = matrices[:, cols].astype(BF16)
            gather.start_z(unit)

    def gather_step(t):
        for unit in (2 * t, 2 * t + 1):
            if t < pairs:
                gather.start_hop(unit, 0)
        if t + ahead < pairs:
            cast_pair(t + ahead)
        if t >= 1:
            for unit in (2 * t - 2, 2 * t - 1):
                gather.start_hop(unit, 1)

    def gather_finish(first, last):
        for unit in range(2 * first, 2 * last):
            gather.finish(unit)

    for pair in range(ahead):
        cast_pair(pair)

    def norm_one(tile, carry):
        unit_x, _ = normalized(tokens[tile].astype(F32))
        act_one[tile] = (unit_x * norm[0:1] + norm[1:2]).astype(BF16)
        return carry + total_rows(cotangent[tile].astype(F32))

    r5 = tiles(norm_one, jnp.zeros((1, D), F32))
    gather_step(0)

    key_index = lax.broadcasted_iota(jnp.int32, (length, length), 0)
    query_index = lax.broadcasted_iota(jnp.int32, (length, length), 1)
    same = key_index == query_index
    slots = task_mask.shape[1]
    slot_same = lax.broadcasted_iota(jnp.int32, (slots, slots), 0) == lax.broadcasted_iota(
        jnp.int32, (slots, slots), 1
    )
    for item in range(items):
        query_ids = group_ids[item : item + 1, :]
        key_ids = jnp.sum(jnp.where(same, query_ids, 0), axis=1, keepdims=True)
        filled = jnp.sum(jnp.where(slot_same, task_mask[item : item + 1, :], 0), axis=1, keepdims=True)
        live = jnp.concatenate([filled, jnp.ones((length - slots, 1), jnp.int32)], axis=0)
        odd_key = jnp.where((key_ids == 0) | (key_ids % 2 == 1), 1, 0)
        earlier = (odd_key == 1) & (key_ids <= query_ids)
        visible = (earlier | (key_ids == query_ids)) & (live == 1)
        caps[item] = jnp.where(visible | same, 3.0e38, NEGATIVE)
    gather_step(1)
    act_one_t[...] = act_one[...].T
    cot_t[...] = cotangent[...].T
    gather_step(2)
    gather_step(3)
    gather_finish(0, 3)

    for item in range(items):
        part = pl.ds(item * length, length)
        for start, scale, bias in ((Q0, HD**-0.5, 0), (K0, 1.0, None), (V0, 1.0, HEAD_COLS)):
            value = rows_dot(act_one[part], weight(start, HEAD_COLS))
            if bias is not None:
                value = value + column[:, bias : bias + HEAD_COLS]
            value = value.astype(BF16)
            if scale != 1.0:
                value = value * jnp.asarray(scale, BF16)
            proj[part, start : start + HEAD_COLS] = value

    head_pairs = HEAD_COLS // 128
    lane = lax.broadcasted_iota(jnp.int32, (length, 128), 1)
    first_half = lane < HD

    def lanes(start, pair):
        return pl.ds(pl.multiple_of(start + pair * 128, 128), 128)

    def attend(item):
        part = pl.ds(item * length, length)

        def one_pair(pair, carry):
            query, key, value = (proj[part, lanes(start, pair)] for start in (Q0, K0, V0))
            sides = []
            for side in range(2):
                own = first_half if side == 0 else ~first_half
                scores = dot_rt(jnp.where(own, key, jnp.zeros_like(key)), query)
                scores = jnp.minimum(scores, caps[item])
                weights = jnp.exp(scores - jnp.max(scores, 0, keepdims=True))
                prob = weights * (1.0 / jnp.sum(weights, 0, keepdims=True))
                probs[item, pair * 2 + side] = prob
                sides.append(dot_lt(prob.astype(BF16), value))
            heads[part, lanes(0, pair)] = jnp.where(first_half, sides[0], sides[1]).astype(BF16)
            return carry

        lax.fori_loop(0, head_pairs, one_pair, 0)

    for item in range(items):
        part = pl.ds(item * length, length)
        attend(item)
        send_part(0, item, dot_rt(heads[part], weight(O0, HEAD_COLS)))
        gather_step(4 + item)
    wait_part(0)

    def norm_two(tile, carry):
        value = tokens[tile].astype(F32) + both(0, tile) + norm[4:5]
        residual[tile] = value
        unit_x, _ = normalized(value)
        act_two[tile] = (unit_x * norm[2:3] + norm[3:4]).astype(BF16)
        return carry

    tiles(norm_two, 0)
    gather_step(6)
    act_two_t[...] = act_two[...].T
    gather_finish(3, 6)

    def up(index, carry):
        start = pl.multiple_of(index * COL_TILE, COL_TILE)
        cols = pl.ds(start, COL_TILE)
        unit = rows_dot(act_two[...], weight(pl.multiple_of(U0 + start, COL_TILE), COL_TILE))
        unit = unit + column[:, pl.ds(pl.multiple_of(2 * HEAD_COLS + start, COL_TILE), COL_TILE)]
        square = unit * unit
        bent = jnp.tanh(unit * (GELU_SCALE + (GELU_SCALE * GELU_CUBIC) * square))
        half = 0.5 * (1.0 + bent)
        hidden[:, cols] = (unit * half).astype(BF16)
        slope[:, cols] = half + 0.5 * unit * (1.0 - bent * bent) * (
            GELU_SCALE + (3.0 * GELU_SCALE * GELU_CUBIC) * square
        )
        return carry

    lax.fori_loop(0, 3, up, 0)
    gather_step(7)
    lax.fori_loop(3, 6, up, 0)
    gather_step(8)

    def down_grad(index, carry):
        start = pl.multiple_of(index * COL_TILE, COL_TILE)
        put_grad(
            pl.multiple_of(W0 + start, COL_TILE), COL_TILE, rows_dot(cot_t[...], hidden[:, pl.ds(start, COL_TILE)])
        )
        return carry

    lax.fori_loop(0, 2, down_grad, 0)
    scatter.begin(1)
    gather_step(9)
    lax.fori_loop(2, 4, down_grad, 0)
    scatter.begin(1)
    lax.fori_loop(4, 6, down_grad, 0)
    scatter.begin(1)
    gather_finish(6, 9)

    def pre_grad(index):
        start = index * COL_TILE
        cols = pl.ds(start, COL_TILE)
        value = rows_dot(cotangent[...], weight(W0 + start, COL_TILE))
        low = (value * slope[:, cols]).astype(BF16)
        grad_pre[:, cols] = low
        row, first = divmod(2 * HEAD_COLS + start, D)
        vectors[6 + row : 7 + row, first : first + COL_TILE] = total_rows(low.astype(F32))
        put_grad(U0 + start, COL_TILE, rows_dot(act_two_t[...], low))

    for index in range(UNIT_COLS // COL_TILE):
        pre_grad(index)
        if index % 2 == 1:
            scatter.begin(1)
        if index in (1, 3, 5):
            scatter.advance()
    for item in range(items):
        part = pl.ds(item * length, length)
        send_part(1, item, dot_rt(grad_pre[part], weight(U0, UNIT_COLS)))
    scatter.advance()
    wait_part(1)

    def norm_two_back(tile, carry):
        gain_sum, shift_sum, res_sum = carry
        incoming = both(1, tile)
        unit_x, scale = normalized(residual[tile])
        pulled = incoming * norm[2:3]
        inner_mean = jnp.mean(pulled, -1, keepdims=True)
        cross_mean = jnp.mean(pulled * unit_x, -1, keepdims=True)
        value = cotangent[tile].astype(F32) + scale * (pulled - inner_mean - unit_x * cross_mean)
        grad_res[tile] = value
        grad_low[tile] = value.astype(BF16)
        return (
            gain_sum + total_rows(incoming * unit_x),
            shift_sum + total_rows(incoming),
            res_sum + total_rows(value),
        )

    zero_row = jnp.zeros((1, D), F32)
    r2g, r2b, r4 = tiles(norm_two_back, (zero_row, zero_row, zero_row))
    scatter.advance()
    put_grad(O0, HEAD_COLS, dot_lt(grad_low[...], heads[...]))
    scatter.begin(1)
    for item in range(items):
        part = pl.ds(item * length, length)
        grad_heads[part] = rows_dot(grad_low[part], weight(O0, HEAD_COLS)).astype(BF16)
    scatter.advance()

    def attend_back(item):
        part = pl.ds(item * length, length)

        def one_pair(pair, carry):
            query, key, value = (proj[part, lanes(start, pair)] for start in (Q0, K0, V0))
            grad = grad_heads[part, lanes(0, pair)]
            sides = []
            for side in range(2):
                own = first_half if side == 0 else ~first_half
                prob = probs[item, pair * 2 + side]
                grad_prob = dot_rt(jnp.where(own, value, jnp.zeros_like(value)), grad)
                inner_sum = jnp.sum(prob * grad_prob, 0, keepdims=True)
                low = (prob * (grad_prob - inner_sum)).astype(BF16)
                sides.append(
                    (dot_lt(low, key) * (HD**-0.5), rows_dot(low, query), rows_dot(prob.astype(BF16), grad))
                )
            for start, left, right in zip((Q0, K0, V0), sides[0], sides[1]):
                grad_proj[part, lanes(start, pair)] = jnp.where(first_half, left, right).astype(BF16)
            return carry

        lax.fori_loop(0, head_pairs, one_pair, 0)

    for item in range(items):
        attend_back(item)
        scatter.advance()

    for item in range(items):
        part = pl.ds(item * length, length)
        send_part(2, item, dot_rt(hidden[part], weight(W0, UNIT_COLS)))
    put_grad(Q0, HEAD_COLS, rows_dot(act_one_t[...], grad_proj[:, Q0 : Q0 + HEAD_COLS]))
    scatter.begin(1)
    put_grad(K0, HEAD_COLS, rows_dot(act_one_t[...], grad_proj[:, K0 : K0 + HEAD_COLS]))
    scatter.begin(1)
    scatter.advance()
    put_grad(V0, HEAD_COLS, rows_dot(act_one_t[...], grad_proj[:, V0 : V0 + HEAD_COLS]))
    scatter.begin(1)
    scatter.advance()
    wait_part(2)
    for item in range(items):
        part = pl.ds(item * length, length)
        send_part(3, item, dot_rt(grad_proj[part], weight(Q0, 3 * HEAD_COLS)))
    r_q = total_rows(grad_proj[:, Q0 : Q0 + HEAD_COLS].astype(F32))
    r_v = total_rows(grad_proj[:, V0 : V0 + HEAD_COLS].astype(F32))

    def finish_out(tile, carry):
        out[tile] = (residual[tile] + both(2, tile) + norm[5:6]).astype(BF16)
        return carry

    tiles(finish_out, 0)
    scatter.advance()
    wait_part(3)

    def norm_one_back(tile, carry):
        gain_sum, shift_sum = carry
        incoming = both(3, tile)
        unit_x, scale = normalized(tokens[tile].astype(F32))
        pulled = incoming * norm[0:1]
        inner_mean = jnp.mean(pulled, -1, keepdims=True)
        cross_mean = jnp.mean(pulled * unit_x, -1, keepdims=True)
        input_grad[tile] = grad_res[tile] + scale * (pulled - inner_mean - unit_x * cross_mean)
        return gain_sum + total_rows(incoming * unit_x), shift_sum + total_rows(incoming)

    r1g, r1b = tiles(norm_one_back, (zero_row, zero_row))
    scatter.advance()

    for row, value in enumerate((r1g, r1b, r2g, r2b, r4, r5)):
        vectors[row : row + 1, :] = value
    vectors[6:7, :HEAD_COLS] = r_q
    vectors[6:7, HEAD_COLS:] = r_v
    for row in range(9, vectors.shape[0]):
        vectors[row : row + 1, :] = zero_row
    for hop, peer in enumerate((place.across_x(), place.across_y())):
        move = remote(vectors, vec_got.at[hop], vs.at[hop], vr.at[hop], peer)
        move.start()
        move.wait()
        vectors[...] = vectors[...] + vec_got[hop]
        scatter.advance()
    vec_z[place.z] = vectors[...]

    def vec_copy(step, owner_z):
        block = vec_z.at[owner_z]
        return remote(block, block, vs.at[1 + step], vr.at[1 + step], place.along_z(step))

    for step in range(1, NZ):
        vec_copy(step, place.z).start()
    scatter.complete()
    for step in range(1, NZ):
        vec_copy(step, (place.z - step) % NZ).wait_recv()
        vec_copy(step, place.z).wait_send()
    vectors[...] = (vec_z[0] + vec_z[1]) + (vec_z[2] + vec_z[3])
    for unit in range(len(GATHER_UNITS)):
        gather.drain(unit)
    for unit in range(len(SCATTER_UNITS)):
        scatter.drain(unit)
    for turn in (2, 3):
        for item in range(items):
            exchange(turn, item).wait_send()


def run_block(inner, tokens, cotangent, task_mask, group_ids, slab, norm_bias, column_bias):
    rows = tokens.shape[0]
    items, length = group_ids.shape
    slab_rows, cols = slab.shape
    heads = HEAD_COLS // HD
    gather_units, scatter_units = len(GATHER_UNITS), len(SCATTER_UNITS)
    dma = pltpu.SemaphoreType.DMA
    vmem = pltpu.VMEM
    in_vmem = pl.BlockSpec(memory_space=pltpu.VMEM)
    return pl.pallas_call(
        functools.partial(block_kernel, inner, items, length),
        out_shape=(
            jax.ShapeDtypeStruct((rows, D), BF16),
            jax.ShapeDtypeStruct((rows, D), F32),
            jax.ShapeDtypeStruct((slab_rows, cols), F32),
            jax.ShapeDtypeStruct((16, D), F32),
        ),
        in_specs=[in_vmem] * 7,
        out_specs=(in_vmem,) * 4,
        scratch_shapes=[
            vmem((NZ, NY, NX, slab_rows, cols), BF16),
            vmem((NZ, NY, NX, slab_rows, cols), BF16),
            vmem((NZ, 2, slab_rows, cols), BF16),
            vmem((NZ, slab_rows, cols), BF16),
            vmem((NZ - 1, slab_rows, cols), BF16),
            vmem((rows, D), BF16),
            vmem((D, rows), BF16),
            vmem((rows, D), BF16),
            vmem((D, rows), BF16),
            vmem((D, rows), BF16),
            vmem((rows, 3 * HEAD_COLS), BF16),
            vmem((rows, 3 * HEAD_COLS), BF16),
            vmem((rows, HEAD_COLS), BF16),
            vmem((rows, HEAD_COLS), BF16),
            vmem((items, length, length), F32),
            vmem((items, heads, length, length), F32),
            vmem((rows, D), F32),
            vmem((rows, UNIT_COLS), F32),
            vmem((rows, UNIT_COLS), BF16),
            vmem((rows, UNIT_COLS), BF16),
            vmem((rows, D), F32),
            vmem((rows, D), BF16),
            vmem((2, rows, D), BF16),
            vmem((2, rows, D), BF16),
            vmem((2, 16, D), F32),
            vmem((NZ, 16, D), F32),
            dma((gather_units, NZ - 1)),
            dma((gather_units, NZ - 1)),
            dma((gather_units, 2)),
            dma((gather_units, 2)),
            dma((scatter_units, 2)),
            dma((scatter_units, 2)),
            dma((scatter_units, NZ - 1)),
            dma((scatter_units, NZ - 1)),
            dma((4, items)),
            dma((4, items)),
            dma((2 + NZ - 1,)),
            dma((2 + NZ - 1,)),
        ],
        compiler_params=pltpu.CompilerParams(
            collective_id=0, has_side_effects=True, vmem_limit_bytes=60 << 20
        ),
    )(tokens, cotangent, task_mask, group_ids, slab, norm_bias, column_bias)


def adam_update(weight_now, gradient, first_now, second_now, step_rate, weight_decay):
    first_new = BETA_FIRST * first_now + (1.0 - BETA_FIRST) * gradient
    second_new = BETA_SECOND * second_now + (1.0 - BETA_SECOND) * gradient * gradient
    first_fixed = first_new / (1.0 - BETA_FIRST**STEP)
    second_fixed = second_new / (1.0 - BETA_SECOND**STEP)
    weight_new = weight_now - step_rate * (
        first_fixed / (jnp.sqrt(second_fixed) + EPS_ADAM) + weight_decay * weight_now
    )
    return (weight_new, first_new, second_new)


def local(
    tokens,
    cotangent,
    task_mask,
    group_ids,
    matrices,
    matrix_first,
    matrix_second,
    matrix_average,
    norm_bias,
    norm_first,
    norm_second,
    norm_average,
    column_bias,
    column_first,
    column_second,
    column_average,
):
    inner = lax.axis_size("dp") // OUTER
    groups = [[outer * inner + i for i in range(inner)] for outer in range(OUTER)]
    slab = matrices
    if inner > 1:
        slab = lax.all_gather(
            matrices.astype(BF16), "dp", axis=0, tiled=True, axis_index_groups=groups
        ).astype(F32)
    output, input_grad, matrix_grad, vectors = run_block(
        inner, tokens, cotangent, task_mask, group_ids, slab, norm_bias, column_bias.reshape(1, -1)
    )
    if inner > 1:
        matrix_grad = lax.psum_scatter(
            matrix_grad, "dp", scatter_dimension=0, tiled=True, axis_index_groups=groups
        )
        vectors = jnp.sum(lax.all_gather(vectors, "dp", axis=0, axis_index_groups=groups), 0)
    norm_grad = vectors[:6]
    column_grad = vectors[6:9].reshape(-1)
    matrix_updated, matrix_moment, matrix_squares = adam_update(
        matrices, matrix_grad, matrix_first, matrix_second, RATE_MATRIX, DECAY_MATRIX
    )
    norm_updated, norm_moment, norm_squares = adam_update(
        norm_bias, norm_grad, norm_first, norm_second, RATE_VECTOR, 0.0
    )
    column_updated, column_moment, column_squares = adam_update(
        column_bias, column_grad, column_first, column_second, RATE_VECTOR, 0.0
    )
    matrix_smoothed = AVERAGE_KEEP * matrix_average + (1.0 - AVERAGE_KEEP) * matrix_updated
    norm_smoothed = AVERAGE_KEEP * norm_average + (1.0 - AVERAGE_KEEP) * norm_updated
    column_smoothed = AVERAGE_KEEP * column_average + (1.0 - AVERAGE_KEEP) * column_updated
    return (
        output,
        input_grad,
        matrix_grad,
        matrix_updated,
        matrix_moment,
        matrix_squares,
        matrix_smoothed,
        norm_grad,
        norm_updated,
        norm_moment,
        norm_squares,
        norm_smoothed,
        column_grad,
        column_updated,
        column_moment,
        column_squares,
        column_smoothed,
    )


def solution(mesh):
    placed = (
        P("dp", None),
        P("dp", None),
        P("dp", None),
        P("dp", None),
        P("dp", "mp"),
        P("dp", "mp"),
        P("dp", "mp"),
        P("dp", "mp"),
        P(),
        P(),
        P(),
        P(),
        P("mp"),
        P("mp"),
        P("mp"),
        P("mp"),
    )
    return jax.shard_map(
        local,
        mesh=mesh,
        in_specs=placed,
        out_specs=(
            P("dp", None),
            P("dp", None),
            P("dp", "mp"),
            P("dp", "mp"),
            P("dp", "mp"),
            P("dp", "mp"),
            P("dp", "mp"),
            P(),
            P(),
            P(),
            P(),
            P(),
            P("mp"),
            P("mp"),
            P("mp"),
            P("mp"),
            P("mp"),
        ),
        check_vma=False,
    )
```

time: 497 us -> 188 us (0.38); the launches traced: 488 us -> 188 us
  waiting for transfers between devices: 280 us -> 0 us
  Pallas kernels: 0 us -> 176 us
  blocking collectives: 79.5 us -> 0 us
  matrix products: 54.9 us -> 0 us
  other arithmetic: 32.9 us -> 5.84 us
  local copies, waits for them, and re-layouts: 25.4 us -> 5.15 us
  between operations: 15.1 us -> 0.81 us
    pallas_call x0 -> x1, Pallas kernels: none -> 176 us  [run_block(): pl.pallas_call(functools.partial(block_kernel, inner, items, length), out...]
    reduce_scatter x1 -> x0, waiting for transfers between devices: 142 us -> none  [local(): lax.psum_scatter(jnp.concatenate([grad_qkv, grad_out, grad_up, grad_down]...]
    all_gather x1 -> x0, waiting for transfers between devices: 104 us -> none  [local(): lax.all_gather(matrices.astype(jnp.bfloat16), 'dp', axis=0, tiled=True)]
    psum x1 -> x0, blocking collectives: 79.5 us -> none  [local(): norm_grad, column_grad = lax.psum((norm_local, column_local), 'dp')]
    dot_general x18 -> x0, matrix products: 54.9 us -> none  [the longest x1 6.42 us: local(): jnp.einsum('rd,rf->df', cotangent, hidden, preferred_element_type=jnp.flo...]
    psum x3 -> x0, waiting for transfers between devices: 33.9 us -> none  [the longest x1 17.4 us: local(): lax.psum(head_part.astype(jnp.bfloat16), 'mp').astype(jnp.float32)]
    squeeze x8 -> x0, local copies, waits for them, and re-layouts: 13.6 us -> none  [local(): lax.map(lambda packed: attend_block(*packed), (blocks(query_low), blocks(...]
    reduce_sum x10 -> x0, other arithmetic: 12.4 us -> none  [the longest x4 6.23 us: layer_norm(): return center * lax.rsqrt(spread + NORM_EPSILON) * gain_row + bias_row]
  transfers between devices with their start and end apart: 5 -> 0, of which waited for: 5 -> 0; matrix products, arithmetic and copies ran while one was open for 7% -> 0% of each run, Pallas kernels for 0% -> 0%
where the time goes in v2:
time: 188 us
  Pallas kernels  176 us (94%)
  other arithmetic  5.84 us (3%)
  local copies, waits for them, and re-layouts  5.15 us (3%)
    pallas_call x1, Pallas kernels, run_block(): pl.pallas_call(functools.partial(block_kernel, inner, items, length), out...  176 us
    add x1, other arithmetic, local(): AVERAGE_KEEP * matrix_average + (1.0 - AVERAGE_KEEP) * matrix_updated  3.81 us

profile of v2, /device:TPU:0, one launch (start us, length us, event | category | flops | bytes accessed | tf_op | source)
XLA Modules:
  0.0 187.9 jit_solution(4184161743085027910)
XLA Ops:
  0.7 0.0 copy-start
  0.7 0.0 copy-start.4
  0.7 0.0 copy-start.5
  0.7 1.5 reshape.40.column
  2.2 176.1 %shard_map.287 = (bf16[576,768]{1,0:T(8,128)(2,1)}, f32[576,768]{1,0:T(8,128)}, f32[48,4608]{1,0:T(8,128)}, f32[16,768]{1,0:T(8,128)}) custom-call(bf16[576,768]{1,0:T(8,128)(2,1)} %tokens.1, bf16[576,768]{1,0:T(8,128)(2,1)} %cotangent.1, s32[2,16]{1,0:T(2,128)} %task_mask.1, s32[2,288]{1,0:T(2,128)} %group_ids.1, f32[48,4608]{1,0:T(8,128)} %matrices.1, ...), custom_call_target="tpu_custom_call" | custom-call | tf_op jit(solution)/shard_map/pallas_call | solution.py:636
  178.3 0.0 copy-done
  178.3 0.0 copy-done.4
  178.3 0.0 copy-done.5
  178.3 0.0 copy-start.6
  178.3 0.0 copy-start.9
  178.3 0.0 copy-start.10
  178.4 0.0 copy-start.11
  178.4 0.0 copy-start.12
  178.4 0.0 copy-start.8
  178.4 0.0 copy-start.3
  178.4 3.8 %multiply_add_fusion = (f32[48,4608]{1,0:T(8,128)}, f32[48,4608]{1,0:T(8,128)}, f32[48,4608]{1,0:T(8,128)}, f32[48,4608]{1,0:T(8,128)}) fusion(f32[48,4608]{1,0:T(8,128)S(1)} %copy-done.4, f32[48,4608]{1,0:T(8,128)S(1)} %copy-done, f32[48,4608]{1,0:T(8,128)} %get-tuple-element.57, f32[48,4608]{1,0:T(8,128)S(1)} %copy-done.5, f32[48,4608]{1,0:T(8,128)} %param.22), kind=kLoop, calls=%fused_computation.2 | loop fusion | flops 3981312 | bytes 7962624 | tf_op jit(solution)/shard_map/add | solution.py:747
  182.2 0.0 copy-start.2
  182.2 0.0 copy-done.6
  182.2 0.0 copy-done.9
  182.2 0.0 copy-done.10
  182.2 0.0 copy-done.11
  182.2 0.0 copy-done.12
  182.2 0.7 multiply_add_fusion.2
  182.9 0.0 copy-done.8
  182.9 0.0 copy-start.7
  182.9 1.4 multiply_add_fusion.4
  184.3 0.0 copy-done.3
  184.3 0.9 copy.36
  185.2 0.0 copy-done.2
  185.2 0.0 copy-start.1
  185.2 1.2 copy.37
  186.4 0.0 copy-done.7
  186.4 0.6 copy-done.1
  187.0 0.9 copy.38
  (2 shorter events, 0.0 us)
Async XLA Ops:
  0.7 177.6 %copy-start = (f32[48,4608]{1,0:T(8,128)S(1)}, f32[48,4608]{1,0:T(8,128)}, u32[]{:S(2)}) copy-start(f32[48,4608]{1,0:T(8,128)} %matrices.1) | copy-start | bytes 2654212
  0.7 177.6 %copy-start.4 = (f32[48,4608]{1,0:T(8,128)S(1)}, f32[48,4608]{1,0:T(8,128)}, u32[]{:S(2)}) copy-start(f32[48,4608]{1,0:T(8,128)} %param.23) | copy-start | bytes 2654212
  0.7 177.6 %copy-start.5 = (f32[48,4608]{1,0:T(8,128)S(1)}, f32[48,4608]{1,0:T(8,128)}, u32[]{:S(2)}) copy-start(f32[48,4608]{1,0:T(8,128)} %param.21) | copy-start | bytes 2654212
  178.3 3.9 %copy-start.6 = (f32[6,768]{1,0:T(8,128)S(1)}, f32[6,768]{1,0:T(8,128)}, u32[]{:S(2)}) copy-start(f32[6,768]{1,0:T(8,128)} %norm.1) | copy-start | bytes 55300
  178.3 3.9 %copy-start.9 = (f32[16,768]{1,0:T(8,128)S(1)}, f32[16,768]{1,0:T(8,128)}, u32[]{:S(2)}) copy-start(f32[16,768]{1,0:T(8,128)} %get-tuple-element.24) | copy-start | bytes 147460
  178.3 3.9 %copy-start.10 = (f32[6,768]{1,0:T(8,128)S(1)}, f32[6,768]{1,0:T(8,128)}, u32[]{:S(2)}) copy-start(f32[6,768]{1,0:T(8,128)} %param.27) | copy-start | bytes 55300
  178.4 3.9 %copy-start.11 = (f32[6,768]{1,0:T(8,128)S(1)}, f32[6,768]{1,0:T(8,128)}, u32[]{:S(2)}) copy-start(f32[6,768]{1,0:T(8,128)} %param.25) | copy-start | bytes 55300
  178.4 3.9 %copy-start.12 = (f32[6,768]{1,0:T(8,128)S(1)}, f32[6,768]{1,0:T(8,128)}, u32[]{:S(2)}) copy-start(f32[6,768]{1,0:T(8,128)} %param.26) | copy-start | bytes 55300
  178.4 4.5 %copy-start.8 = (f32[2304]{0:T(1024)S(1)}, f32[2304]{0:T(1024)}, u32[]{:S(2)}) copy-start(f32[2304]{0:T(1024)} %param.28) | copy-start | bytes 27652
  178.4 5.9 %copy-start.3 = (bf16[576,768]{1,0:T(8,128)(2,1)S(1)}, bf16[576,768]{1,0:T(8,128)(2,1)}, u32[]{:S(2)}) copy-start(bf16[576,768]{1,0:T(8,128)(2,1)} %get-tuple-element.55) | copy-start | bytes 2654212
  182.2 3.0 %copy-start.2 = (f32[576,768]{1,0:T(8,128)S(1)}, f32[576,768]{1,0:T(8,128)}, u32[]{:S(2)}) copy-start(f32[576,768]{1,0:T(8,128)} %get-tuple-element.56) | copy-start | bytes 5308420
  182.9 3.5 %copy-start.7 = (f32[2304]{0:T(1024)}, f32[2304]{0:T(1024)S(1)}, u32[]{:S(2)}) copy-start(f32[2304]{0:T(1024)S(1)} %reshape.41) | copy-start | bytes 27652
  185.2 1.8 copy-start.1
